TPU v7x, 32 devices: a whole 2x2x4 slice. The times are simulated.
32 devices in a mesh: section: 2 (over core), dp: 4 (over y, x), ctx: 4 (over z).
Axes of the slice: x: 2, y: 2, z: 4, core: 2. Of those that a mesh axis runs over, the one named last changes fastest.
Arguments:
- tokens: bfloat16 [16, 512, 768], P('dp', 'ctx'), may hold values from -6 to 6
- segment_ids: int32 [16, 512], P('dp', 'ctx'), may hold values from 0 to 4, as said below
- padding: int32 [16, 512], P('dp', 'ctx'), may hold values from 0 to 1, as said below
- dropped: int32 [2, 16], P('section', 'dp'), may hold values 0 or 1
- qkv_weight: bfloat16 [2, 768, 2304], P('section'), may hold values from -0.21875 to 0.21875
- query_bias: float32 [2, 768], P('section'), may hold values from -1.75 to 1.75
- value_bias: float32 [2, 768], P('section'), may hold values from -0.0625 to 0.0625
- attn_weight: bfloat16 [2, 768, 768], P('section'), may hold values from -3.5 to 3.5
- attn_bias: float32 [2, 768], P('section'), may hold values from -1.25 to 1.25
- attn_gain: float32 [2, 768], P('section'), may hold values from 0.5 to 1.5
- attn_shift: float32 [2, 768], P('section'), may hold values from -1.25 to 1.25
- inner_weight: bfloat16 [2, 768, 3072], P('section'), may hold values from -0.21875 to 0.21875
- inner_bias: float32 [2, 3072], P('section'), may hold values from -1.75 to 1.75
- outer_weight: bfloat16 [2, 3072, 768], P('section'), may hold values from -0.109375 to 0.109375
- outer_bias: float32 [2, 768], P('section'), may hold values from -1.25 to 1.25
- ffn_gain: float32 [2, 768], P('section'), may hold values from 0.5 to 1.5
- ffn_shift: float32 [2, 768], P('section'), may hold values from -1.25 to 1.25
- cotangent: bfloat16 [16, 512, 768], P('dp', 'ctx'), may hold values from -6 to 6
Outputs:
- encoded: bfloat16 [16, 512, 768], P('dp', 'ctx', 'section')
- tokens_grad: bfloat16 [16, 512, 768], P('dp', 'ctx', 'section')
- grad_qkv_weight: float32 [2, 768, 2304], P('section', 'dp', 'ctx')
- grad_query_bias: float32 [2, 768], P('section')
- grad_value_bias: float32 [2, 768], P('section')
- grad_attn_weight: float32 [2, 768, 768], P('section', 'dp', 'ctx')
- grad_attn_bias: float32 [2, 768], P('section')
- grad_attn_gain: float32 [2, 768], P('section')
- grad_attn_shift: float32 [2, 768], P('section')
- grad_inner_weight: float32 [2, 768, 3072], P('section', 'dp', 'ctx')
- grad_inner_bias: float32 [2, 3072], P('section')
- grad_outer_weight: float32 [2, 3072, 768], P('section', 'dp', 'ctx')
- grad_outer_bias: float32 [2, 768], P('section')
- grad_ffn_gain: float32 [2, 768], P('section')
- grad_ffn_shift: float32 [2, 768], P('section')
Inputs may be any that keep to these rules, and one draw needn't show every extreme that they name: `segment_ids`: ids never fall along a row; every row holds exactly the documents 0 to 4. `padding`: 1 on a prefix of each row, 0 on the rest; every row has padded positions, all inside document 4, which keeps at least one real token.
All inputs are finite; a program needn't handle non-finite values. No bound on the sum of `dropped` on one device may be relied on, other than what follows from the above.
Results may differ from a plain program's by a relative error of at most 0.034.
Values may be sent and summed in bfloat16 or wider, within the bound.
No kernel may reach another device: no remote copies, remote signals or barrier semaphores. Data moves between devices by JAX's collectives and lax.ppermute only.
A program may use at most 256 MiB of HBM per device.

v0:
```python
from functools import partial

import jax
import jax.numpy as jnp
from jax import lax
from jax.sharding import PartitionSpec as P

HEADS = 12
HEAD_DIM = 64


norm_eps = 1e-05
masked_score = -1e30


def shifted(x, axis, by):
    length = lax.axis_size(axis)
    return lax.ppermute(x, axis, [(i, (i + by) % length) for i in range(length)])


def matmul_low(left, right):
    return jnp.dot(left, right, preferred_element_type=jnp.float32)


def left_product(left, right):
    return jnp.einsum("ti,to->io", left, right, preferred_element_type=jnp.float32)


def right_product(left, right):
    return jnp.einsum("to,io->ti", left, right, preferred_element_type=jnp.float32)


def normalize(values):
    mean_value = jnp.mean(values, axis=-1, keepdims=True)
    centered = values - mean_value
    variance = jnp.mean(centered * centered, axis=-1, keepdims=True)
    inverse = lax.rsqrt(variance + norm_eps)
    return (centered * inverse, inverse)


def norm_back(grad_out, normed, inverse, gain):
    scaled = grad_out * gain
    return inverse * (
        scaled
        - jnp.mean(scaled, axis=-1, keepdims=True)
        - normed * jnp.mean(scaled * normed, axis=-1, keepdims=True)
    )


def attend_piece(query_heads, seg_query, running, pieces):
    run_max, run_total, run_acc = running
    key_piece, value_piece, seg_piece, pad_piece = pieces
    count = key_piece.shape[0]
    key_heads = key_piece.reshape(count, HEADS, HEAD_DIM)
    value_heads = value_piece.reshape(count, HEADS, HEAD_DIM)
    scores = jnp.einsum(
        "qhd,khd->hqk", query_heads, key_heads, preferred_element_type=jnp.float32
    ) * HEAD_DIM ** (-0.5)
    allowed = (seg_query[:, None] == seg_piece[None, :]) & (pad_piece[None, :] == 1)
    scores = jnp.where(allowed[None], scores, masked_score)
    new_max = jnp.maximum(run_max, jnp.max(scores, axis=-1))
    weights = jnp.where(allowed[None], jnp.exp(scores - new_max[..., None]), 0.0)
    run_total = jnp.sum(weights, axis=-1)
    run_acc = jnp.einsum(
        "hqk,khd->hqd",
        weights.astype(jnp.bfloat16),
        value_heads,
        preferred_element_type=jnp.float32,
    )
    return (new_max, run_total, run_acc)


def attention_back(
    query_low, key_all, value_all, seg_query, seg_all, pad_all, log_total, row_delta, grad_att
):
    row_count = query_low.shape[0]
    seq_count = key_all.shape[0]
    score_scale = HEAD_DIM ** (-0.5)
    query_heads = query_low.reshape(row_count, HEADS, HEAD_DIM)
    key_heads = key_all.reshape(seq_count, HEADS, HEAD_DIM)
    value_heads = value_all.reshape(seq_count, HEADS, HEAD_DIM)
    grad_heads = grad_att.reshape(row_count, HEADS, HEAD_DIM)
    scores = (
        jnp.einsum("qhd,khd->hqk", query_heads, key_heads, preferred_element_type=jnp.float32)
        * score_scale
    )
    allowed = (seg_query[:, None] == seg_all[None, :]) & (pad_all[None, :] == 1)
    prob_rows = jnp.where(allowed[None], jnp.exp(scores - log_total[..., None]), 0.0)
    grad_probs = jnp.einsum(
        "qhd,khd->hqk", grad_heads, value_heads, preferred_element_type=jnp.float32
    )
    grad_scores = (prob_rows * (grad_probs - row_delta[..., None])).astype(jnp.bfloat16)
    grad_query = (
        jnp.einsum("hqk,khd->qhd", grad_scores, key_heads, preferred_element_type=jnp.float32)
        * score_scale
    )
    grad_key = (
        jnp.einsum("hqk,qhd->khd", grad_scores, query_heads, preferred_element_type=jnp.float32)
        * score_scale
    )
    grad_value = jnp.einsum(
        "hqk,qhd->khd",
        prob_rows.astype(jnp.bfloat16),
        grad_heads,
        preferred_element_type=jnp.float32,
    )
    model_width = HEADS * HEAD_DIM
    return (
        grad_query.reshape(row_count, model_width),
        grad_key.reshape(seq_count, model_width),
        grad_value.reshape(seq_count, model_width),
    )


def layer_forward(layer_input, params, seg_query, pad_query, drop_flag):
    (
        qkv_weight,
        query_bias,
        value_bias,
        attn_weight,
        attn_bias,
        attn_gain,
        attn_shift,
        inner_weight,
        inner_bias,
        outer_weight,
        outer_bias,
        ffn_gain,
        ffn_shift,
    ) = params
    model_width = layer_input.shape[1]
    row_count = layer_input.shape[0]
    projected = matmul_low(layer_input, qkv_weight)
    query_low = (projected[:, :model_width] + query_bias).astype(jnp.bfloat16)
    key_local = projected[:, model_width : 2 * model_width].astype(jnp.bfloat16)
    value_local = (projected[:, 2 * model_width :] + value_bias).astype(jnp.bfloat16)
    query_heads = query_low.reshape(row_count, HEADS, HEAD_DIM)
    start_state = (
        jnp.full((HEADS, row_count), masked_score, jnp.float32),
        jnp.zeros((HEADS, row_count), jnp.float32),
        jnp.zeros((HEADS, row_count, HEAD_DIM), jnp.float32),
    )
    key_all, value_all, seg_all, pad_all = (
        lax.all_gather(key_local, "ctx", axis=0, tiled=True),
        lax.all_gather(value_local, "ctx", axis=0, tiled=True),
        lax.all_gather(seg_query, "ctx", axis=0, tiled=True),
        lax.all_gather(pad_query, "ctx", axis=0, tiled=True),
    )
    run_max, run_total, run_acc = attend_piece(
        query_heads, seg_query, start_state, (key_all, value_all, seg_all, pad_all)
    )
    gathered = (key_all, value_all, seg_all, pad_all)
    attended = (run_acc / run_total[..., None]).transpose(1, 0, 2).reshape(row_count, model_width)
    log_total = run_max + jnp.log(run_total)
    branch = matmul_low(attended.astype(jnp.bfloat16), attn_weight) + attn_bias
    sum_attn = layer_input.astype(jnp.float32) + branch
    normed, inverse = normalize(sum_attn)
    first_norm = normed * attn_gain + attn_shift
    inner_pre = matmul_low(first_norm.astype(jnp.bfloat16), inner_weight) + inner_bias
    active_low = jax.nn.gelu(inner_pre, approximate=False).astype(jnp.bfloat16)
    sum_ffn = first_norm + matmul_low(active_low, outer_weight) + outer_bias
    normed_two, inverse_two = normalize(sum_ffn)
    result = normed_two * ffn_gain + ffn_shift
    result = jnp.where(drop_flag > 0, layer_input.astype(jnp.float32), result)
    kept_items = (
        layer_input,
        query_low,
        key_local,
        value_local,
        attended,
        log_total,
        sum_attn,
        inner_pre,
        sum_ffn,
    ) + gathered
    return (result, kept_items)


def layer_backward(grad_out, kept_items, params, seg_query):
    (
        qkv_weight,
        query_bias,
        value_bias,
        attn_weight,
        attn_bias,
        attn_gain,
        attn_shift,
        inner_weight,
        inner_bias,
        outer_weight,
        outer_bias,
        ffn_gain,
        ffn_shift,
    ) = params
    (
        layer_input,
        query_low,
        key_local,
        value_local,
        attended,
        log_total,
        sum_attn,
        inner_pre,
        sum_ffn,
    ) = kept_items[:9]
    model_width = layer_input.shape[1]
    row_count = layer_input.shape[0]
    normed, inverse = normalize(sum_attn)
    first_norm = normed * attn_gain + attn_shift
    normed_two, inverse_two = normalize(sum_ffn)
    grad_ffn_gain = jnp.sum(grad_out * normed_two, axis=0)
    grad_ffn_shift = jnp.sum(grad_out, axis=0)
    grad_sum_ffn = norm_back(grad_out, normed_two, inverse_two, ffn_gain)
    grad_ffn_low = grad_sum_ffn.astype(jnp.bfloat16)
    active, gelu_pull = jax.vjp(partial(jax.nn.gelu, approximate=False), inner_pre)
    grad_outer_weight = left_product(active.astype(jnp.bfloat16), grad_ffn_low)
    grad_outer_bias = jnp.sum(grad_ffn_low.astype(jnp.float32), axis=0)
    grad_active = right_product(grad_ffn_low, outer_weight)
    grad_inner = gelu_pull(grad_active)[0].astype(jnp.bfloat16)
    grad_inner_weight = left_product(first_norm.astype(jnp.bfloat16), grad_inner)
    grad_inner_bias = jnp.sum(grad_inner.astype(jnp.float32), axis=0)
    grad_first = grad_sum_ffn + right_product(grad_inner, inner_weight)
    grad_attn_gain = jnp.sum(grad_first * normed, axis=0)
    grad_attn_shift = jnp.sum(grad_first, axis=0)
    grad_sum_attn = norm_back(grad_first, normed, inverse, attn_gain)
    grad_branch = grad_sum_attn.astype(jnp.bfloat16)
    grad_attn_weight = left_product(attended.astype(jnp.bfloat16), grad_branch)
    grad_attn_bias = jnp.sum(grad_branch.astype(jnp.float32), axis=0)
    grad_attended = right_product(grad_branch, attn_weight).astype(jnp.bfloat16)
    key_all, value_all, seg_all, pad_all = kept_items[9:]
    row_delta = jnp.sum(
        (grad_attended.astype(jnp.float32) * attended).reshape(row_count, HEADS, HEAD_DIM), axis=-1
    ).T
    grad_query, grad_key_all, grad_value_all = attention_back(
        query_low,
        key_all,
        value_all,
        seg_query,
        seg_all,
        pad_all,
        log_total,
        row_delta,
        grad_attended,
    )
    grad_key, grad_value = (
        lax.psum_scatter(
            grad_key_all.astype(jnp.bfloat16), "ctx", scatter_dimension=0, tiled=True
        ).astype(jnp.float32),
        lax.psum_scatter(
            grad_value_all.astype(jnp.bfloat16), "ctx", scatter_dimension=0, tiled=True
        ).astype(jnp.float32),
    )
    grad_qkv = jnp.concatenate([grad_query, grad_key, grad_value], axis=1).astype(jnp.bfloat16)
    grad_qkv_weight = left_product(layer_input, grad_qkv)
    grad_query_bias = jnp.sum(grad_qkv[:, :model_width].astype(jnp.float32), axis=0)
    grad_value_bias = jnp.sum(grad_qkv[:, 2 * model_width :].astype(jnp.float32), axis=0)
    grad_input = grad_sum_attn + right_product(grad_qkv, qkv_weight)
    layer_grads = (
        grad_qkv_weight,
        grad_query_bias,
        grad_value_bias,
        grad_attn_weight,
        grad_attn_bias,
        grad_attn_gain,
        grad_attn_shift,
        grad_inner_weight,
        grad_inner_bias,
        grad_outer_weight,
        grad_outer_bias,
        grad_ffn_gain,
        grad_ffn_shift,
    )
    return (layer_grads, grad_input)


def body(
    tokens,
    segment_ids,
    padding,
    dropped,
    qkv_weight,
    query_bias,
    value_bias,
    attn_weight,
    attn_bias,
    attn_gain,
    attn_shift,
    inner_weight,
    inner_bias,
    outer_weight,
    outer_bias,
    ffn_gain,
    ffn_shift,
    cotangent,
):
    micro_count = tokens.shape[0]
    section_index = lax.axis_index("section")
    half_width = tokens.shape[2] // lax.axis_size("section")
    params = tuple(
        (
            member[0]
            for member in (
                qkv_weight,
                query_bias,
                value_bias,
                attn_weight,
                attn_bias,
                attn_gain,
                attn_shift,
                inner_weight,
                inner_bias,
                outer_weight,
                outer_bias,
                ffn_gain,
                ffn_shift,
            )
        )
    )
    drop_row = dropped[0]
    incoming = jnp.zeros(tokens.shape[1:], jnp.bfloat16)
    saved_ticks = []
    encoded_rows = []
    for tick_index in range(micro_count + 1):
        micro_index = jnp.clip(tick_index - section_index, 0, micro_count - 1)
        own_input = lax.dynamic_index_in_dim(tokens, micro_index, 0, False)
        layer_input = jnp.where(section_index == 0, own_input, incoming)
        seg_query = lax.dynamic_index_in_dim(segment_ids, micro_index, 0, False)
        pad_query = lax.dynamic_index_in_dim(padding, micro_index, 0, False)
        drop_flag = lax.dynamic_index_in_dim(drop_row, micro_index, 0, False)
        layer_out, kept_items = layer_forward(layer_input, params, seg_query, pad_query, drop_flag)
        layer_low = layer_out.astype(jnp.bfloat16)
        received = shifted(layer_low, "section", 1)
        incoming = received
        if tick_index >= 1:
            encoded_rows.append(jnp.where(section_index == 0, received, layer_low))
        saved_ticks.append(kept_items)
    stacked = jax.tree.map(lambda *members: jnp.stack(members), *saved_ticks)
    grad_totals = tuple((jnp.zeros(member.shape, jnp.float32) for member in params))
    grad_incoming = jnp.zeros(tokens.shape[1:], jnp.bfloat16)
    input_rows = []
    for tick_index in range(micro_count + 1):
        raw_index = tick_index - 1 + section_index
        micro_index = jnp.clip(raw_index, 0, micro_count - 1)
        live_tick = ((raw_index >= 0) & (raw_index < micro_count)).astype(jnp.float32)
        forward_tick = jnp.clip(tick_index - 1 + 2 * section_index, 0, micro_count)
        kept_items = jax.tree.map(
            lambda member: lax.dynamic_index_in_dim(member, forward_tick, 0, False), stacked
        )
        own_cot = lax.dynamic_index_in_dim(cotangent, micro_index, 0, False)
        upstream = jnp.where(section_index == 1, own_cot, grad_incoming).astype(jnp.float32)
        seg_query = lax.dynamic_index_in_dim(segment_ids, micro_index, 0, False)
        pad_query = lax.dynamic_index_in_dim(padding, micro_index, 0, False)
        drop_flag = lax.dynamic_index_in_dim(drop_row, micro_index, 0, False)
        keep_scale = (drop_flag == 0).astype(jnp.float32) * live_tick
        layer_grads, grad_input = layer_backward(
            upstream * keep_scale, kept_items, params, seg_query
        )
        grad_totals = tuple((total + term for total, term in zip(grad_totals, layer_grads)))
        grad_input = grad_input + (drop_flag > 0).astype(jnp.float32) * upstream
        grad_low = grad_input.astype(jnp.bfloat16)
        received = shifted(grad_low, "section", 1)
        grad_incoming = received
        if tick_index >= 1:
            input_rows.append(jnp.where(section_index == 0, grad_low, received))
    reduced_once = (
        lax.psum_scatter(
            grad_totals[0][None].astype(jnp.bfloat16), "dp", scatter_dimension=1, tiled=True
        ).astype(jnp.float32),
        lax.psum_scatter(
            grad_totals[3][None].astype(jnp.bfloat16), "dp", scatter_dimension=1, tiled=True
        ).astype(jnp.float32),
        lax.psum_scatter(
            grad_totals[7][None].astype(jnp.bfloat16), "dp", scatter_dimension=1, tiled=True
        ).astype(jnp.float32),
        lax.psum_scatter(
            grad_totals[9][None].astype(jnp.bfloat16), "dp", scatter_dimension=1, tiled=True
        ).astype(jnp.float32),
    )
    matrix_grads = (
        lax.psum_scatter(
            reduced_once[0].astype(jnp.bfloat16), "ctx", scatter_dimension=2, tiled=True
        ).astype(jnp.float32),
        lax.psum_scatter(
            reduced_once[1].astype(jnp.bfloat16), "ctx", scatter_dimension=2, tiled=True
        ).astype(jnp.float32),
        lax.psum_scatter(
            reduced_once[2].astype(jnp.bfloat16), "ctx", scatter_dimension=2, tiled=True
        ).astype(jnp.float32),
        lax.psum_scatter(
            reduced_once[3].astype(jnp.bfloat16), "ctx", scatter_dimension=2, tiled=True
        ).astype(jnp.float32),
    )
    vector_grads = lax.psum(
        (
            grad_totals[1][None],
            grad_totals[2][None],
            grad_totals[4][None],
            grad_totals[5][None],
            grad_totals[6][None],
            grad_totals[8][None],
            grad_totals[10][None],
            grad_totals[11][None],
            grad_totals[12][None],
        ),
        ("dp", "ctx"),
    )
    encoded = lax.dynamic_slice_in_dim(
        jnp.stack(encoded_rows), section_index * half_width, half_width, 2
    )
    tokens_grad = lax.dynamic_slice_in_dim(
        jnp.stack(input_rows), section_index * half_width, half_width, 2
    )
    return (
        encoded,
        tokens_grad,
        matrix_grads[0],
        vector_grads[0],
        vector_grads[1],
        matrix_grads[1],
        vector_grads[2],
        vector_grads[3],
        vector_grads[4],
        matrix_grads[2],
        vector_grads[5],
        matrix_grads[3],
        vector_grads[6],
        vector_grads[7],
        vector_grads[8],
    )


def solution(mesh):
    placed = (
        P("dp", "ctx", None),
        P("dp", "ctx"),
        P("dp", "ctx"),
        P("section", "dp"),
        P("section", None, None),
        P("section", None),
        P("section", None),
        P("section", None, None),
        P("section", None),
        P("section", None),
        P("section", None),
        P("section", None, None),
        P("section", None),
        P("section", None, None),
        P("section", None),
        P("section", None),
        P("section", None),
        P("dp", "ctx", None),
    )
    return jax.shard_map(
        body,
        mesh=mesh,
        in_specs=placed,
        out_specs=(
            P("dp", "ctx", "section"),
            P("dp", "ctx", "section"),
            P("section", "dp", "ctx"),
            P("section", None),
            P("section", None),
            P("section", "dp", "ctx"),
            P("section", None),
            P("section", None),
            P("section", None),
            P("section", "dp", "ctx"),
            P("section", None),
            P("section", "dp", "ctx"),
            P("section", None),
            P("section", None),
            P("section", None),
        ),
        check_vma=False,
    )
```

profile of v0, /device:TPU:0, one launch (start us, length us, event | category | flops | bytes accessed | tf_op | source)
XLA Modules:
  0.0 1240.4 jit_solution(15255078155460408472)
XLA Ops:
  11.1 12.5 %all-gather = s32[1,512]{1,0:T(1,128)S(1)} all-gather(s32[1,128]{1,0:T(1,128)S(1)} %get-tuple-element.212), channel_id=2, replica_groups=mesh['section'=2,'dp'=4,'ctx'=4] {'ctx'}, dimensions={1}, use_global_device_ids=true | all-gather | bytes 2560 | tf_op jit(solution)/shard_map/all_gather | solution.py:146
  25.0 7.5 all-gather.1
  39.6 18.7 %all_gather.62 = bf16[512,768]{1,0:T(8,128)(2,1)} all-gather(bf16[128,768]{1,0:T(8,128)(2,1)} %slice.129), channel_id=1, replica_groups=mesh['section'=2,'dp'=4,'ctx'=4] {'ctx'}, dimensions={0}, use_global_device_ids=true | all-gather | bytes 983040 | tf_op jit(solution)/shard_map/all_gather | solution.py:144
  66.6 16.4 %all_gather.63 = bf16[512,768]{1,0:T(8,128)(2,1)} all-gather(bf16[128,768]{1,0:T(8,128)(2,1)S(1)} %fusion.752), channel_id=1, replica_groups=mesh['section'=2,'dp'=4,'ctx'=4] {'ctx'}, dimensions={0}, use_global_device_ids=true | all-gather | bytes 983040 | tf_op jit(solution)/shard_map/all_gather | solution.py:145
  96.5 4.5 bitcast_dynamic-update-slice_fusion.4
  101.0 6.2 fusion.1124
  116.0 9.5 all-gather.3
  126.6 7.5 all-gather.5
  135.3 9.5 all-gather.7
  145.9 7.5 all-gather.9
  156.0 9.8 all-gather.2
  166.4 9.1 all-gather.4
  176.2 9.0 all-gather.6
  185.9 9.1 all-gather.8
  216.3 17.9 %all_gather.66 = bf16[512,768]{1,0:T(8,128)(2,1)} all-gather(bf16[128,768]{1,0:T(8,128)(2,1)} %slice.128), channel_id=1, replica_groups=mesh['section'=2,'dp'=4,'ctx'=4] {'ctx'}, dimensions={0}, use_global_device_ids=true | all-gather | bytes 983040 | tf_op jit(solution)/shard_map/all_gather | solution.py:144
  241.3 16.4 %all_gather.67 = bf16[512,768]{1,0:T(8,128)(2,1)} all-gather(bf16[128,768]{1,0:T(8,128)(2,1)S(1)} %copy-done.129), channel_id=1, replica_groups=mesh['section'=2,'dp'=4,'ctx'=4] {'ctx'}, dimensions={0}, use_global_device_ids=true | all-gather | bytes 983040 | tf_op jit(solution)/shard_map/all_gather | solution.py:145
  268.4 4.1 fusion.1127
  284.2 19.6 %all_gather.70 = bf16[512,768]{1,0:T(8,128)(2,1)} all-gather(bf16[128,768]{1,0:T(8,128)(2,1)} %slice.127), channel_id=1, replica_groups=mesh['section'=2,'dp'=4,'ctx'=4] {'ctx'}, dimensions={0}, use_global_device_ids=true | all-gather | bytes 983040 | tf_op jit(solution)/shard_map/all_gather | solution.py:144
  306.2 3.6 fusion.80
  311.0 18.7 %all_gather.71 = bf16[512,768]{1,0:T(8,128)(2,1)} all-gather(bf16[128,768]{1,0:T(8,128)(2,1)S(1)} %copy-done.130), channel_id=1, replica_groups=mesh['section'=2,'dp'=4,'ctx'=4] {'ctx'}, dimensions={0}, use_global_device_ids=true | all-gather | bytes 983040 | tf_op jit(solution)/shard_map/all_gather | solution.py:145
  340.4 4.1 fusion.1130
  356.2 19.1 %all_gather.74 = bf16[512,768]{1,0:T(8,128)(2,1)} all-gather(bf16[128,768]{1,0:T(8,128)(2,1)} %slice.126), channel_id=1, replica_groups=mesh['section'=2,'dp'=4,'ctx'=4] {'ctx'}, dimensions={0}, use_global_device_ids=true | all-gather | bytes 983040 | tf_op jit(solution)/shard_map/all_gather | solution.py:144
  377.6 3.6 fusion.81
  382.4 18.5 %all_gather.75 = bf16[512,768]{1,0:T(8,128)(2,1)} all-gather(bf16[128,768]{1,0:T(8,128)(2,1)S(1)} %copy-done.131), channel_id=1, replica_groups=mesh['section'=2,'dp'=4,'ctx'=4] {'ctx'}, dimensions={0}, use_global_device_ids=true | all-gather | bytes 983040 | tf_op jit(solution)/shard_map/all_gather | solution.py:145
  411.5 4.1 fusion.1133
  427.3 19.1 %all_gather.78 = bf16[512,768]{1,0:T(8,128)(2,1)} all-gather(bf16[128,768]{1,0:T(8,128)(2,1)} %slice.125), channel_id=1, replica_groups=mesh['section'=2,'dp'=4,'ctx'=4] {'ctx'}, dimensions={0}, use_global_device_ids=true | all-gather | bytes 983040 | tf_op jit(solution)/shard_map/all_gather | solution.py:144
  453.6 18.3 %all_gather.79 = bf16[512,768]{1,0:T(8,128)(2,1)} all-gather(bf16[128,768]{1,0:T(8,128)(2,1)S(1)} %copy-done.128), channel_id=1, replica_groups=mesh['section'=2,'dp'=4,'ctx'=4] {'ctx'}, dimensions={0}, use_global_device_ids=true | all-gather | bytes 983040 | tf_op jit(solution)/shard_map/all_gather | solution.py:145
  483.2 7.5 bitcast_dynamic-update-slice_fusion.15
  497.0 7.1 convert_reduce_fusion.4
  504.2 4.5 multiply_reduce_fusion.4
  526.3 6.4 constant_dynamic-slice_fusion.1
  581.1 11.1 reduce-scatter.55.cloned.1.call-done
  602.6 8.2 convert_reduce_fusion.3
  610.9 4.1 multiply_reduce_fusion.3
  654.9 18.5 %reduce-scatter.59.cloned.1.call-done = bf16[128,768]{1,0:T(8,128)(2,1)} async-done(((bf16[512,768]{1,0:T(8,128)(2,1)}), bf16[128,768]{1,0:T(8,128)(2,1)}) %reduce-scatter.59.cloned.1.call-update) | async-done | bytes 196624
  683.3 8.2 convert_reduce_fusion.2
  691.5 3.7 multiply_reduce_fusion.2
  736.6 17.0 %reduce-scatter.63.cloned.1.call-done = bf16[128,768]{1,0:T(8,128)(2,1)} async-done(((bf16[512,768]{1,0:T(8,128)(2,1)}), bf16[128,768]{1,0:T(8,128)(2,1)}) %reduce-scatter.63.cloned.1.call-update) | async-done | bytes 196624
  763.5 8.2 convert_reduce_fusion.1
  771.7 3.7 multiply_reduce_fusion.1
  819.8 14.3 %reduce-scatter.67.cloned.1.call-done = bf16[128,768]{1,0:T(8,128)(2,1)} async-done(((bf16[512,768]{1,0:T(8,128)(2,1)}), bf16[128,768]{1,0:T(8,128)(2,1)}) %reduce-scatter.67.cloned.1.call-update) | async-done | bytes 196624
  844.8 8.2 convert_reduce_fusion
  853.0 3.7 multiply_reduce_fusion
  861.7 3.7 fusion.331
  889.2 5.4 fusion.780
  894.6 4.0 fusion.777
  898.7 3.9 fusion.774
  902.7 4.1 fusion.771
  909.8 5.4 reduce-scatter.71.cloned.1.call-done
  916.9 13.1 %fusion.40 = bf16[1,768,2304]{2,1,0:T(8,128)(2,1)} fusion(f32[768,2304]{1,0:T(8,128)} %fusion.771, f32[768,2304]{1,0:T(8,128)} %fusion.774, f32[768,2304]{1,0:T(8,128)} %fusion.780, f32[768,2304]{1,0:T(8,128)} %fusion.777, bf16[128,768]{0,1:T(8,128)(2,1)} %copy.175, bf16[128,768]{0,1:T(8,128)(2,1)} %copy.173, bf16[128,768]{0,1:T(8,128)(2,1)} %bitcast.1324, ...), kind=kOutput, calls=%fused_computation.43 | convolution fusion | flops 463601664 | bytes 32636932 | tf_op jit(solution)/shard_map/ti,to->io/dot_general | solution.py:26
  930.7 9.9 fusion.482
  940.6 9.7 fusion.475
  950.3 10.0 fusion.477
  960.3 9.8 fusion.479
  970.1 17.9 %fusion.42 = bf16[1,3072,768]{2,1,0:T(8,128)(2,1)} fusion(f32[3072,768]{1,0:T(8,128)} %fusion.479, f32[3072,768]{1,0:T(8,128)} %fusion.477, f32[3072,768]{1,0:T(8,128)} %fusion.482, f32[3072,768]{1,0:T(8,128)} %fusion.475, f32[5,128,3072]{2,1,0:T(8,128)} %get-tuple-element.277, s32[]{:T(128)S(6)} %min.59, f32[128,768]{1,0:T(8,128)S(1)} %copy-done.111), kind=kOutput, calls=%fused_computation.45 | convolution fusion | flops 641433600 | bytes 44433412 | tf_op jit(solution)/shard_map/ti,to->io/dot_general | solution.py:26
  988.7 6.5 fusion.786
  995.2 6.3 fusion.787
  1001.5 6.5 fusion.788
  1008.0 6.2 fusion.789
  1014.2 17.6 %fusion.41 = bf16[1,768,3072]{2,1,0:T(8,128)(2,1)} fusion(bf16[128,3072]{1,0:T(8,128)(2,1)} %copy-done.80, f32[768,3072]{1,0:T(8,128)} %fusion.789, f32[768,3072]{1,0:T(8,128)} %fusion.788, f32[768,3072]{1,0:T(8,128)} %fusion.786, f32[768,3072]{1,0:T(8,128)} %fusion.787, f32[768]{0:T(1024)S(1)} %copy-done.84, f32[768]{0:T(1024)S(1)} %reduce.15, ...), kind=kOutput, calls=%fused_computation.44 | convolution fusion | flops 616267776 | bytes 43654148 | tf_op jit(solution)/shard_map/ti,to->io/dot_general | solution.py:26
  1036.9 6.2 copy.176
  1056.3 6.6 copy.180
  1076.3 40.0 %reduce-scatter.49.cloned.1.call-done = bf16[1,192,3072]{2,1,0:T(8,128)(2,1)} async-done(((bf16[1,768,3072]{2,1,0:T(8,128)(2,1)}), bf16[1,192,3072]{2,1,0:T(8,128)(2,1)}) %reduce-scatter.49.cloned.1.call-update) | async-done | bytes 1179664 | tf_op jit(solution)/shard_map/reduce_scatter | solution.py:372
  1131.2 79.7 %all-reduce = (f32[1,768]{1,0:T(1,128)}, f32[1,768]{1,0:T(1,128)}, f32[1,768]{1,0:T(1,128)}, f32[1,768]{1,0:T(1,128)}, f32[1,768]{1,0:T(1,128)}, /*index=5*/f32[...) all-reduce(f32[1,768]{1,0:T(1,128)S(1)} %copy-done.231, ...), channel_id=1, replica_groups=mesh['section'=2,'dp'=4,'ctx'=4] {'dp','ctx'}, use_global_device_ids=true, to_apply=%region_92.93 | all-reduce | flops 9216 | bytes 73728 | tf_op jit(solution)/shard_map/psum | solution.py:393
  (1076 shorter events, 502.3 us)
Async XLA Ops:
  7.2 27.2 %copy-start = (bf16[1,768,2304]{2,1,0:T(8,128)(2,1)S(1)}, bf16[1,768,2304]{2,1,0:T(8,128)(2,1)}, u32[]{:S(2)}) copy-start(bf16[1,768,2304]{2,1,0:T(8,128)(2,1)} %param.22) | copy-start | bytes 10616836
  7.2 572.2 %reduce-scatter.57.cloned.1.call-start = ((), (), s32[]{:S(2)}) async-start(), calls=%async_computation.24 | async-start | bytes 983040
  9.4 82.8 %copy-start.151 = (f32[768]{0:T(1024)}, f32[768]{0:T(1024)S(1)}, u32[]{:S(2)}) copy-start(f32[768]{0:T(1024)S(1)} %reduce.14) | copy-start | bytes 9220
  23.6 37.0 %copy-start.183 = (s32[1,512]{1,0:T(1,128)}, s32[1,512]{1,0:T(1,128)S(1)}, u32[]{:S(2)}) copy-start(s32[1,512]{1,0:T(1,128)S(1)} %all-gather) | copy-start | bytes 6148
  37.8 22.8 %copy-start.271 = (pred[512]{0:T(512)(128)(4,1)S(1)}, pred[512]{0:T(512)(128)(4,1)}, u32[]{:S(2)}) copy-start(pred[512]{0:T(512)(128)(4,1)} %compare_reduce_fusion.4) | copy-start | bytes 1540
  65.6 19.8 %copy-start.161 = (f32[768]{0:T(1024)}, f32[768]{0:T(1024)S(1)}, u32[]{:S(2)}) copy-start(f32[768]{0:T(1024)S(1)} %reduce.13) | copy-start | bytes 9220
  65.6 19.8 %copy-start.263 = (f32[1,768]{1,0:T(1,128)S(1)}, f32[1,768]{1,0:T(1,128)}, u32[]{:S(2)}) copy-start(f32[1,768]{1,0:T(1,128)} %param.28) | copy-start | bytes 9220
  85.4 397.8 %copy-start.83 = (f32[768]{0:T(1024)}, f32[768]{0:T(1024)S(1)}, u32[]{:S(2)}) copy-start(f32[768]{0:T(1024)S(1)} %reduce.16) | copy-start | bytes 9220
  109.7 100.4 %collective-permute-start = (bf16[128,768]{1,0:T(8,128)(2,1)}, bf16[128,768]{1,0:T(8,128)(2,1)}, u32[]{:S(2)}, u32[]{:S(2)}) collective-permute-start(bf16[128,768]{1,0:T(8,128)(2,1)} %fusion.704), channel_id=1, source_target_pairs={{0,16},{16,0},{1,17},{17,1},{2,18},{18,2},{3,19},{19,3},{4,20},{20... | collective-permute-start | bytes 589832 | tf_op jit(solution)/shard_map/ppermute | solution.py:18
  112.9 13.7 %copy-start.274 = (s32[1,128]{1,0:T(1,128)S(1)}, s32[1,128]{1,0:T(1,128)}, u32[]{:S(2)}) copy-start(s32[1,128]{1,0:T(1,128)} %get-tuple-element.215) | copy-start | bytes 1540
  112.9 22.4 %copy-start.273 = (s32[1,128]{1,0:T(1,128)S(1)}, s32[1,128]{1,0:T(1,128)}, u32[]{:S(2)}) copy-start(s32[1,128]{1,0:T(1,128)} %get-tuple-element.218) | copy-start | bytes 1540
  112.9 33.0 %copy-start.272 = (s32[1,128]{1,0:T(1,128)S(1)}, s32[1,128]{1,0:T(1,128)}, u32[]{:S(2)}) copy-start(s32[1,128]{1,0:T(1,128)} %get-tuple-element.214) | copy-start | bytes 1540
  272.9 5.0 collective-permute-start.1
  344.9 4.9 collective-permute-start.2
  416.1 5.0 collective-permute-start.3
  483.2 13.8 %slice-start.22 = ((s8[4718592]{0:T(1024)(128)(4,1)}), s8[4194304]{0:T(1024)(128)(4,1)S(1)}, s32[]{:S(2)}) async-start(s8[4718592]{0:T(1024)(128)(4,1)} %bitcast.1427), calls=%async_computation.58 | async-start | bytes 8388608
  483.2 13.8 %slice-start.23 = ((s8[4718592]{0:T(1024)(128)(4,1)}), s8[524288]{0:T(1024)(128)(4,1)S(1)}, s32[]{:S(2)}) async-start(s8[4718592]{0:T(1024)(128)(4,1)} %bitcast.1427), calls=%async_computation.59 | async-start | bytes 1048576
  493.8 10.3 copy-start.245
  494.0 10.1 copy-start.264
  494.0 19.0 %copy-start.220 = (f32[128]{0:T(128)}, f32[128]{0:T(128)S(1)}, u32[]{:S(2)}) copy-start(f32[128]{0:T(128)S(1)} %broadcast_multiply_fusion.27) | copy-start | bytes 1540
  543.9 48.4 %reduce-scatter.55.cloned.1.call-start = ((), (), s32[]{:S(2)}) async-start(), calls=%async_computation.23 | async-start | bytes 983040
  562.7 90.5 %reduce-scatter.61.cloned.1.call-start = ((), (), s32[]{:S(2)}) async-start(), calls=%async_computation.26 | async-start | bytes 983040
  563.3 34.9 %copy-start.247 = (f32[128]{0:T(128)}, f32[128]{0:T(128)S(1)}, u32[]{:S(2)}) copy-start(f32[128]{0:T(128)S(1)} %broadcast_multiply_fusion.10) | copy-start | bytes 1540
  594.0 16.8 %slice-start.8 = ((s8[4718592]{0:T(1024)(128)(4,1)}), s8[4194304]{0:T(1024)(128)(4,1)S(1)}, s32[]{:S(2)}) async-start(s8[4718592]{0:T(1024)(128)(4,1)} %bitcast.1291), calls=%async_computation.44 | async-start | bytes 8388608
  596.7 1.5 collective-permute-start.5
  596.8 13.9 %copy-start.228 = (f32[128]{0:T(128)}, f32[128]{0:T(128)S(1)}, u32[]{:S(2)}) copy-start(f32[128]{0:T(128)S(1)} %broadcast_multiply_fusion.17) | copy-start | bytes 1540
  625.9 47.5 %reduce-scatter.59.cloned.1.call-start = ((), (), s32[]{:S(2)}) async-start(), calls=%async_computation.25 | async-start | bytes 983040
  640.3 94.5 %reduce-scatter.65.cloned.1.call-start = ((), (), s32[]{:S(2)}) async-start(), calls=%async_computation.28 | async-start | bytes 983040
  675.1 16.3 %slice-start.10 = ((s8[4718592]{0:T(1024)(128)(4,1)}), s8[4194304]{0:T(1024)(128)(4,1)S(1)}, s32[]{:S(2)}) async-start(s8[4718592]{0:T(1024)(128)(4,1)} %bitcast.1293), calls=%async_computation.46 | async-start | bytes 8388608
  677.9 1.5 collective-permute-start.6
  678.0 17.2 %copy-start.238 = (f32[128]{0:T(128)}, f32[128]{0:T(128)S(1)}, u32[]{:S(2)}) copy-start(f32[128]{0:T(128)S(1)} %add_rsqrt_fusion.5) | copy-start | bytes 1540
  706.2 47.5 %reduce-scatter.63.cloned.1.call-start = ((), (), s32[]{:S(2)}) async-start(), calls=%async_computation.27 | async-start | bytes 983040
  720.3 97.7 %reduce-scatter.69.cloned.1.call-start = ((), (), s32[]{:S(2)}) async-start(), calls=%async_computation.30 | async-start | bytes 983040
  755.3 16.3 %slice-start.12 = ((s8[4718592]{0:T(1024)(128)(4,1)}), s8[4194304]{0:T(1024)(128)(4,1)S(1)}, s32[]{:S(2)}) async-start(s8[4718592]{0:T(1024)(128)(4,1)} %bitcast.1295), calls=%async_computation.48 | async-start | bytes 8388608
  758.1 1.5 collective-permute-start.7
  758.2 17.2 %copy-start.240 = (f32[128]{0:T(128)}, f32[128]{0:T(128)S(1)}, u32[]{:S(2)}) copy-start(f32[128]{0:T(128)S(1)} %add_rsqrt_fusion.3) | copy-start | bytes 1540
  786.4 47.6 %reduce-scatter.67.cloned.1.call-start = ((), (), s32[]{:S(2)}) async-start(), calls=%async_computation.29 | async-start | bytes 983040
  800.5 107.6 %reduce-scatter.73.cloned.1.call-start = ((), (), s32[]{:S(2)}) async-start(), calls=%async_computation.32 | async-start | bytes 983040
  835.8 17.2 %slice-start.14 = ((s8[4718592]{0:T(1024)(128)(4,1)}), s8[4194304]{0:T(1024)(128)(4,1)S(1)}, s32[]{:S(2)}) async-start(s8[4718592]{0:T(1024)(128)(4,1)} %bitcast.1297), calls=%async_computation.50 | async-start | bytes 8388608
  838.6 1.5 collective-permute-start.8
  838.7 18.0 %copy-start.251 = (f32[128]{0:T(128)}, f32[128]{0:T(128)S(1)}, u32[]{:S(2)}) copy-start(f32[128]{0:T(128)S(1)} %add_rsqrt_fusion.1) | copy-start | bytes 1540
  867.8 47.4 %reduce-scatter.71.cloned.1.call-start = ((), (), s32[]{:S(2)}) async-start(), calls=%async_computation.31 | async-start | bytes 983040
  882.3 149.6 %reduce-scatter.47.cloned.1.call-start = ((), (), s32[]{:S(2)}) async-start(), calls=%async_computation.19 | async-start | bytes 1474560 | tf_op jit(solution)/shard_map/reduce_scatter | solution.py:369
  889.1 147.8 %reduce-scatter.45.cloned.1.call-start = ((), (), s32[]{:S(2)}) async-start(), calls=%async_computation.18 | async-start | bytes 4423680 | tf_op jit(solution)/shard_map/reduce_scatter | solution.py:366
  930.1 126.2 %reduce-scatter.53.cloned.1.call-start = ((), (), s32[]{:S(2)}) async-start(), calls=%async_computation.22 | async-start | bytes 5898240 | tf_op jit(solution)/shard_map/reduce_scatter | solution.py:375
  988.0 128.2 %reduce-scatter.49.cloned.1.call-start = ((), (), s32[]{:S(2)}) async-start(), calls=%async_computation.20 | async-start | bytes 5898240 | tf_op jit(solution)/shard_map/reduce_scatter | solution.py:372
  1031.9 181.8 %reduce-scatter.77.cloned.1.call-start = ((), (), s32[]{:S(2)}) async-start(), calls=%async_computation.34 | async-start | bytes 491520
  1036.8 181.8 %reduce-scatter.75.cloned.1.call-start = ((), (), s32[]{:S(2)}) async-start(), calls=%async_computation.33 | async-start | bytes 1474560
  1046.0 178.4 %reduce-scatter.79.cloned.1.call-start = ((), (), s32[]{:S(2)}) async-start(), calls=%async_computation.35 | async-start | bytes 1474560
  1065.8 10.2 copy-start.189
  1065.8 10.3 copy-start.192
  1065.8 10.3 copy-start.191
  1065.9 165.4 %reduce-scatter.51.cloned.1.call-start = ((), (), s32[]{:S(2)}) async-start(), calls=%async_computation.21 | async-start | bytes 1474560 | tf_op jit(solution)/shard_map/reduce_scatter | solution.py:386
  1066.1 10.1 copy-start.194
  1066.1 10.1 copy-start.199
  1066.2 10.1 copy-start.202
  1066.2 10.1 copy-start.205
  1074.0 51.6 %collective-permute-start.4 = (bf16[128,768]{1,0:T(8,128)(2,1)}, bf16[128,768]{1,0:T(8,128)(2,1)}, u32[]{:S(2)}, u32[]{:S(2)}) collective-permute-start(bf16[128,768]{1,0:T(8,128)(2,1)} %get-tuple-element.203), channel_id=1, source_target_pairs={{0,16},{16,0},{1,17},{17,1},{2,18},{18,2},{3,19},{19,3},{4,20},{20... | collective-permute-start | bytes 589832 | tf_op jit(solution)/shard_map/ppermute | solution.py:18
  1116.2 12.1 copy-start.47
  1116.2 12.1 copy-start.86
  1116.3 12.1 copy-start.87
  1116.3 12.1 copy-start.113
  1116.3 12.1 copy-start.133
  1130.4 80.5 %collective-permute-start.9 = (bf16[128,768]{1,0:T(8,128)(2,1)}, bf16[128,768]{1,0:T(8,128)(2,1)}, u32[]{:S(2)}, u32[]{:S(2)}) collective-permute-start(bf16[128,768]{1,0:T(8,128)(2,1)} %fusion.737), channel_id=1, source_target_pairs={{0,16},{16,0},{1,17},{17,1},{2,18},{18,2},{3,19},{19,3},{4,20},{20... | collective-permute-start | bytes 589832 | tf_op jit(solution)/shard_map/ppermute | solution.py:18
  (279 other events, 1161.0 us)
Sparse Core Ops, SparseCore 0:
  544.0 23.2 reduce-scatter.56
  569.6 22.5 reduce-scatter.54
  626.0 22.5 reduce-scatter.60
  650.8 22.5 reduce-scatter.58
  706.3 22.5 reduce-scatter.64
  731.0 22.5 reduce-scatter.62
  786.5 22.5 reduce-scatter.68
  811.5 22.5 reduce-scatter.66
  867.9 22.5 reduce-scatter.72
  892.6 22.5 reduce-scatter.70
  918.1 27.7 reduce-scatter.46
  948.8 47.2 reduce-scatter.44
  999.1 57.0 reduce-scatter.52
  1059.1 57.0 reduce-scatter.48
  1118.9 20.6 reduce-scatter.76
  1141.9 28.2 reduce-scatter.74
  1172.4 28.5 reduce-scatter.78
  1203.3 27.9 reduce-scatter.50
where the time goes:
time: 1260 us; the launch traced here: 1240 us
  matrix products  356 us (28%)
  blocking collectives  353 us (28%)
  local copies, waits for them, and re-layouts  239 us (19%)
  other arithmetic  148 us (12%)
  waiting for transfers between devices  113 us (9%)
  between operations  27.5 us (2%)
    dot_general x20, matrix products, left_product(): jnp.einsum('ti,to->io', left, right, preferred_element_type=jnp.float32)  136 us
    unnamed x683, local copies, waits for them, and re-layouts  114 us
    all_gather x5, blocking collectives, layer_forward(): lax.all_gather(key_local, 'ctx', axis=0, tiled=True)  94.5 us
    all_gather x5, blocking collectives, layer_forward(): lax.all_gather(value_local, 'ctx', axis=0, tiled=True)  88.2 us
    dot_general x20, matrix products, right_product(): jnp.einsum('to,io->ti', left, right, preferred_element_type=jnp.float32)  80.5 us
    psum x1, blocking collectives, body(): lax.psum((grad_totals[1][None], grad_totals[2][None], grad_totals[4][None...  79.7 us
    unnamed x31, waiting for transfers between devices  66.6 us
    dynamic_slice x24, local copies, waits for them, and re-layouts, body(): lax.dynamic_index_in_dim(member, forward_tick, 0, False)  52.9 us
  transfers between devices with their start and end apart: 28, of which 11 were waited for; matrix products, arithmetic and copies ran while one was open for 31% of the time, Pallas kernels for 0%

commit v1 on v0

--- a/solution.py
+++ b/solution.py
@@ -3,6 +3,8 @@
 import jax
 import jax.numpy as jnp
 from jax import lax
+from jax.experimental import pallas as pl
+from jax.experimental.pallas import tpu as pltpu
 from jax.sharding import PartitionSpec as P
 
 HEADS = 12
@@ -429,6 +431,709 @@
     )
 
 
+def dot_plain(left, right):
+    return lax.dot_general(left, right, (((1,), (0,)), ((), ())), preferred_element_type=jnp.float32)
+
+
+def dot_flipped(left, right):
+    return lax.dot_general(left, right, (((1,), (1,)), ((), ())), preferred_element_type=jnp.float32)
+
+
+def gelu_parts(x):
+    below = 0.5 * (1.0 + lax.erf(x * 0.7071067811865476))
+    density = jnp.exp(-0.5 * x * x) * 0.3989422804014327
+    return (x * below, below + x * density)
+
+
+def rows_of(index, size):
+    return pl.ds(pl.multiple_of(index * size, size), size)
+
+
+def piece_rows(ctx, at, count, n_pieces):
+    return pl.ds(0, count) if n_pieces == 1 else rows_of(ctx ^ at, count)
+
+
+def head_lanes(shape, which):
+    lane = lax.broadcasted_iota(jnp.int32, shape, 1)
+    return (lane < HEAD_DIM) if which == 0 else (lane >= HEAD_DIM)
+
+
+def mask_into(mask_ref, code_ref, seg_ref):
+    mask_ref[...] = jnp.where(code_ref[...] == seg_ref[...], 0.0, masked_score)
+
+
+def copy_list(pairs, sems, first=0):
+    copies = [pltpu.make_async_copy(src, dst, sems.at[first + at]) for at, (src, dst) in enumerate(pairs)]
+    for copy in copies:
+        copy.start()
+    return copies
+
+
+def forward_kernel(active, n_pieces, n_alias, scal, seg_ref, code_ref, qkv_bias_ref, qkv_scale_ref, vec_ref, inner_bias_ref, *refs):
+    pieces = refs[:n_pieces]
+    wqkv_h, wattn_h, win_h, wout_h = refs[n_pieces : n_pieces + 4]
+    outs = refs[n_pieces + 4 + n_alias :]
+    u_h, qkv_h, att_h, lse_h, n1_h, r1_h, first_h, dg_h, n2_h, r2_h, res_h = outs[:11]
+    (wqkv, wattn, win, wout, u, qkv, att, lse, n1, r1, flow, dg, n2, r2, res, first, acc, mask, sems) = outs[11:]
+    size, width = u.shape
+    hidden = win.shape[1]
+
+    @pl.when(scal[0] == active)
+    def _():
+        count = size // n_pieces
+        ctx = scal[1]
+        start = copy_list(
+            [
+                (piece, u.at[piece_rows(ctx, at, count, n_pieces)]) for at, piece in enumerate(pieces)
+            ]
+            + [(wqkv_h, wqkv), (wattn_h, wattn), (win_h, win), (wout_h, wout)],
+            sems,
+        )
+        mask_into(mask, code_ref, seg_ref)
+        for copy in start[: n_pieces + 1]:
+            copy.wait()
+
+        def project(at, carry):
+            cols = rows_of(at, 256)
+            value = dot_plain(u[...], wqkv[:, cols]) + qkv_bias_ref[:, cols]
+            qkv[:, cols] = (value * qkv_scale_ref[:, cols]).astype(jnp.bfloat16)
+            return carry
+
+        lax.fori_loop(0, 3 * width // 256, project, 0)
+
+        def heads(at, carry):
+            cols = [rows_of(at + part * (width // 128), 128) for part in range(3)]
+            query, key, value = (qkv[:, col] for col in cols)
+            value_t = value.T
+            both = []
+            for which in range(2):
+                key_own = jnp.where(head_lanes(key.shape, which), key, jnp.zeros_like(key))
+                scores = dot_flipped(key_own, query) + mask[...]
+                top = jnp.max(scores, axis=0, keepdims=True)
+                weights = jnp.exp(scores - top)
+                total = jnp.sum(weights, axis=0, keepdims=True)
+                lse[pl.ds(2 * at + which, 1), :] = top + jnp.log(total)
+                part = value_t[which * HEAD_DIM : (which + 1) * HEAD_DIM]
+                both.append(dot_plain(part, weights.astype(jnp.bfloat16)) / total)
+            att[:, cols[0]] = jnp.concatenate(both, axis=0).T.astype(jnp.bfloat16)
+            return carry
+
+        lax.fori_loop(0, width // 128, heads, 0)
+        out_copies = copy_list([(u, u_h), (qkv, qkv_h), (att, att_h), (lse, lse_h)], sems, n_pieces + 4)
+        start[n_pieces + 1].wait()
+
+        def branch(at, carry):
+            cols = rows_of(at, 256)
+            first[:, cols] = dot_plain(att[...], wattn[:, cols])
+            return carry
+
+        lax.fori_loop(0, width // 256, branch, 0)
+
+        def norm_one(at, carry):
+            rows = rows_of(at, 64)
+            value = u[rows].astype(jnp.float32) + first[rows] + vec_ref[0:1, :]
+            normed, inverse = normalize(value)
+            n1[rows] = normed
+            r1[rows] = jnp.broadcast_to(inverse, (64, 128))
+            value = normed * vec_ref[1:2, :] + vec_ref[2:3, :]
+            first[rows] = value
+            flow[rows] = value.astype(jnp.bfloat16)
+            return carry
+
+        lax.fori_loop(0, size // 64, norm_one, 0)
+        out_copies += copy_list([(n1, n1_h), (r1, r1_h), (flow, first_h)], sems, n_pieces + 8)
+        start[n_pieces + 2].wait()
+        start[n_pieces + 3].wait()
+        acc[...] = first[...] + vec_ref[3:4, :]
+
+        def feed(at, carry):
+            cols = rows_of(at, 512)
+            inner = dot_plain(flow[...], win[:, cols]) + inner_bias_ref[:, cols]
+            active_value, slope = gelu_parts(inner)
+            dg[:, cols] = slope.astype(jnp.bfloat16)
+            acc[...] += dot_plain(active_value.astype(jnp.bfloat16), wout[cols, :])
+            return carry
+
+        lax.fori_loop(0, hidden // 512, feed, 0)
+        dropped = scal[2]
+
+        def norm_two(at, carry):
+            rows = rows_of(at, 64)
+            normed, inverse = normalize(acc[rows])
+            n2[rows] = normed
+            r2[rows] = jnp.broadcast_to(inverse, (64, 128))
+            value = normed * vec_ref[4:5, :] + vec_ref[5:6, :]
+            value = jnp.where(dropped > 0, u[rows].astype(jnp.float32), value)
+            res[rows] = value.astype(jnp.bfloat16)
+            return carry
+
+        lax.fori_loop(0, size // 64, norm_two, 0)
+        out_copies += copy_list([(dg, dg_h), (n2, n2_h), (r2, r2_h), (res, res_h)], sems, n_pieces + 11)
+        for copy in out_copies:
+            copy.wait()
+
+
+def kernel_call(body, out_shapes, scratch, operands, n_smem, n_vmem, aliases=None, flops=0, nbytes=0):
+    specs = (
+        [pl.BlockSpec(memory_space=pltpu.SMEM)] * n_smem
+        + [pl.BlockSpec(memory_space=pltpu.VMEM)] * n_vmem
+        + [pl.BlockSpec(memory_space=pl.ANY)] * (len(operands) - n_smem - n_vmem)
+    )
+    return pl.pallas_call(
+        body,
+        out_shape=out_shapes,
+        in_specs=specs,
+        out_specs=jax.tree.map(lambda s: pl.BlockSpec(memory_space=pl.ANY), out_shapes),
+        scratch_shapes=scratch,
+        input_output_aliases=aliases or {},
+        cost_estimate=pl.CostEstimate(flops=flops, bytes_accessed=nbytes, transcendentals=0),
+        compiler_params=pltpu.CompilerParams(vmem_limit_bytes=60 * 2**20),
+    )(*operands)
+
+
+def run_forward(active, scal, seg_row, code_col, small, pieces, weights, earlier):
+    qkv_bias, qkv_scale, vecs, inner_bias = small
+    wqkv, wattn, win, wout = weights
+    width, hidden = win.shape
+    size = seg_row.shape[1]
+    low, full = jnp.bfloat16, jnp.float32
+    outs = [
+        jax.ShapeDtypeStruct(shape, kind)
+        for shape, kind in (
+            ((size, width), low),
+            ((size, 3 * width), low),
+            ((size, width), low),
+            ((16, size), full),
+            ((size, width), full),
+            ((size, 128), full),
+            ((size, width), low),
+            ((size, hidden), low),
+            ((size, width), full),
+            ((size, 128), full),
+            ((size, width), low),
+        )
+    ]
+    scratch = (
+        [pltpu.VMEM(w.shape, low) for w in weights]
+        + [pltpu.VMEM(out.shape, out.dtype) for out in outs]
+        + [
+            pltpu.VMEM((size, width), full),
+            pltpu.VMEM((size, width), full),
+            pltpu.VMEM((size, size), full),
+            pltpu.SemaphoreType.DMA((len(pieces) + 15,)),
+        ]
+    )
+    operands = [scal, seg_row, code_col, qkv_bias, qkv_scale, vecs, inner_bias, *pieces, *weights, *earlier]
+    at_alias = len(operands) - len(earlier)
+    body = partial(forward_kernel, active, len(pieces), len(earlier))
+    return kernel_call(
+        body, outs, scratch, operands, 1, 6, {at_alias + i: i for i in range(len(earlier))}, 8 * 10**9, 10**7
+    )
+
+
+def top_kernel(active, n_pieces, n_alias, scal, vec_ref, *refs):
+    pieces = refs[:n_pieces]
+    n2_h, r2_h = refs[n_pieces : n_pieces + 2]
+    outs = refs[n_pieces + 2 + n_alias :]
+    inc_h, dffn_h, dsum_h, vec_h = outs[:4]
+    inc, dffn, dsum, vec, n2, r2, sems = outs[4:]
+    size, width = inc.shape
+
+    @pl.when(scal[0] == active)
+    def _():
+        count = size // n_pieces
+        ctx = scal[1]
+        start = copy_list(
+            [
+                (piece, inc.at[piece_rows(ctx, at, count, n_pieces)]) for at, piece in enumerate(pieces)
+            ]
+            + [(n2_h, n2), (r2_h, r2)],
+            sems,
+        )
+        for copy in start:
+            copy.wait()
+        keep = jnp.where(scal[2] > 0, 0.0, 1.0)
+        vec[...] = jnp.zeros_like(vec)
+
+        def step(at, carry):
+            rows = rows_of(at, 64)
+            grad = inc[rows].astype(jnp.float32) * keep
+            normed = n2[rows]
+            value = norm_back(grad, normed, r2[rows][:, :1], vec_ref[4:5, :])
+            dsum[rows] = value
+            low = value.astype(jnp.bfloat16)
+            dffn[rows] = low
+            vec[0:1, :] += jnp.sum(low.astype(jnp.float32), axis=0, keepdims=True)
+            vec[1:2, :] += jnp.sum(grad * normed, axis=0, keepdims=True)
+            vec[2:3, :] += jnp.sum(grad, axis=0, keepdims=True)
+            return carry
+
+        lax.fori_loop(0, size // 64, step, 0)
+        for copy in copy_list([(inc, inc_h), (dffn, dffn_h), (dsum, dsum_h), (vec, vec_h)], sems, n_pieces + 2):
+            copy.wait()
+
+
+def run_top(active, scal, vecs, pieces, n2, r2, earlier):
+    size, width = n2.shape
+    low, full = jnp.bfloat16, jnp.float32
+    outs = [
+        jax.ShapeDtypeStruct((size, width), low),
+        jax.ShapeDtypeStruct((size, width), low),
+        jax.ShapeDtypeStruct((size, width), full),
+        jax.ShapeDtypeStruct((8, width), full),
+    ]
+    scratch = [pltpu.VMEM(out.shape, out.dtype) for out in outs] + [
+        pltpu.VMEM((size, width), full),
+        pltpu.VMEM((size, 128), full),
+        pltpu.SemaphoreType.DMA((len(pieces) + 6,)),
+    ]
+    operands = [scal, vecs, *pieces, n2, r2, *earlier]
+    at_alias = len(operands) - len(earlier)
+    body = partial(top_kernel, active, len(pieces), len(earlier))
+    return kernel_call(
+        body, outs, scratch, operands, 1, 1, {at_alias + i: i for i in range(len(earlier))}, 10**7, 10**7
+    )
+
+
+def chain_kernel(active, n_alias, scal, seg_ref, code_ref, vec_ref, *refs):
+    ins, rest = refs[:15], refs[15 + n_alias :]
+    inc_h, dffn_h, dsum_h, dg_h, n1_h, r1_h, att_h, qkv_h, lse_h = ins[:9]
+    wqkv_h, wattn_h, win_h, wout_h = ins[9:13]
+    dqkv_h, dbranch_h, din_h, vec_h = rest[:4]
+    (dqkv, dbranch, din, vec, inc, dffn, dsum, dg, n1, r1, qkv, lse, wqkv, wattn, win, wout, first, datt, mask, sems) = rest[4:]
+    size, width = inc.shape
+    hidden = win.shape[1]
+
+    @pl.when(scal[0] == active)
+    def _():
+        start = copy_list(
+            [
+                (dffn_h, dffn),
+                (wout_h, wout),
+                (dg_h, dg),
+                (win_h, win),
+                (dsum_h, dsum),
+                (n1_h, n1),
+                (r1_h, r1),
+                (wattn_h, wattn),
+                (qkv_h, qkv),
+                (lse_h, lse),
+                (wqkv_h, wqkv),
+                (inc_h, inc),
+            ],
+            sems,
+        )
+        mask_into(mask, code_ref, seg_ref)
+        vec[...] = jnp.zeros_like(vec)
+        for copy in start[:3]:
+            copy.wait()
+
+        def inner(at, carry):
+            cols = rows_of(at, width)
+            grad = dot_flipped(dffn[...], wout[cols, :]) * dg[:, cols].astype(jnp.float32)
+            low = grad.astype(jnp.bfloat16)
+            dg[:, cols] = low
+            vec[pl.ds(8 + at, 1), :] = jnp.sum(low.astype(jnp.float32), axis=0, keepdims=True)
+            return carry
+
+        lax.fori_loop(0, hidden // width, inner, 0)
+        start[3].wait()
+
+        def outer(at, carry):
+            cols = rows_of(at, 256)
+            first[:, cols] = dot_flipped(dg[...], win[cols, :])
+            return carry
+
+        lax.fori_loop(0, width // 256, outer, 0)
+        for copy in start[4:8]:
+            copy.wait()
+
+        def norm_step(at, carry):
+            rows = rows_of(at, 64)
+            grad = first[rows] + dsum[rows]
+            normed = n1[rows]
+            value = norm_back(grad, normed, r1[rows][:, :1], vec_ref[1:2, :])
+            dsum[rows] = value
+            low = value.astype(jnp.bfloat16)
+            dbranch[rows] = low
+            vec[2:3, :] += jnp.sum(low.astype(jnp.float32), axis=0, keepdims=True)
+            vec[3:4, :] += jnp.sum(grad * normed, axis=0, keepdims=True)
+            vec[4:5, :] += jnp.sum(grad, axis=0, keepdims=True)
+            return carry
+
+        lax.fori_loop(0, size // 64, norm_step, 0)
+
+        def attended(at, carry):
+            cols = rows_of(at, 256)
+            datt[:, cols] = dot_flipped(dbranch[...], wattn[cols, :]).astype(jnp.bfloat16)
+            return carry
+
+        lax.fori_loop(0, width // 256, attended, 0)
+        for copy in start[8:10]:
+            copy.wait()
+
+        def heads(at, carry):
+            cols = [rows_of(at + part * (width // 128), 128) for part in range(3)]
+            query, key, value = (qkv[:, col] for col in cols)
+            grad = datt[:, cols[0]]
+            key_t = key.T
+            parts = []
+            for which in range(2):
+                own = head_lanes(key.shape, which)
+                key_own = jnp.where(own, key, jnp.zeros_like(key))
+                value_own = jnp.where(own, value, jnp.zeros_like(value))
+                scores = dot_flipped(key_own, query) + mask[...]
+                probs = jnp.exp(scores - lse[pl.ds(2 * at + which, 1), :])
+                dprobs = dot_flipped(value_own, grad)
+                delta = jnp.sum(probs * dprobs, axis=0, keepdims=True)
+                dscores = (probs * (dprobs - delta)).astype(jnp.bfloat16)
+                parts.append(
+                    (
+                        dot_plain(key_t[which * HEAD_DIM : (which + 1) * HEAD_DIM], dscores),
+                        dot_plain(dscores, query),
+                        dot_plain(probs.astype(jnp.bfloat16), grad),
+                    )
+                )
+            low_lanes = head_lanes((size, 128), 0)
+            dquery = jnp.concatenate([parts[0][0], parts[1][0]], axis=0).T * HEAD_DIM ** (-0.5)
+            dkey = jnp.where(low_lanes, parts[0][1], parts[1][1])
+            dvalue = jnp.where(low_lanes, parts[0][2], parts[1][2])
+            dquery = dquery.astype(jnp.bfloat16)
+            dvalue = dvalue.astype(jnp.bfloat16)
+            dqkv[:, cols[0]] = dquery
+            dqkv[:, cols[1]] = dkey.astype(jnp.bfloat16)
+            dqkv[:, cols[2]] = dvalue
+            vec[0:1, cols[0]] = jnp.sum(dquery.astype(jnp.float32), axis=0, keepdims=True)
+            vec[1:2, cols[0]] = jnp.sum(dvalue.astype(jnp.float32), axis=0, keepdims=True)
+            return carry
+
+        lax.fori_loop(0, width // 128, heads, 0)
+        out_copies = copy_list([(dqkv, dqkv_h), (dbranch, dbranch_h), (vec, vec_h)], sems, 12)
+        for copy in start[10:]:
+            copy.wait()
+        dropped = scal[2]
+
+        def back(at, carry):
+            cols = rows_of(at, 256)
+            value = dsum[:, cols] + dot_flipped(dqkv[...], wqkv[cols, :])
+            value = jnp.where(dropped > 0, inc[:, cols].astype(jnp.float32), value)
+            din[:, cols] = value.astype(jnp.bfloat16)
+            return carry
+
+        lax.fori_loop(0, width // 256, back, 0)
+        out_copies += copy_list([(din, din_h)], sems, 15)
+        for copy in out_copies:
+            copy.wait()
+
+
+def run_chain(active, scal, seg_row, code_col, vecs, top, kept, weights, earlier):
+    u, qkv, att, lse, n1, r1, first, dg, n2, r2, res = kept
+    inc, dffn, dsum, vec = top
+    wqkv, wattn, win, wout = weights
+    size, width = u.shape
+    low, full = jnp.bfloat16, jnp.float32
+    outs = [
+        jax.ShapeDtypeStruct((size, 3 * width), low),
+        jax.ShapeDtypeStruct((size, width), low),
+        jax.ShapeDtypeStruct((size, width), low),
+        jax.ShapeDtypeStruct((16, width), full),
+    ]
+    held = [inc, dffn, dsum, dg, n1, r1, qkv, lse, *weights]
+    scratch = (
+        [pltpu.VMEM(out.shape, out.dtype) for out in outs]
+        + [pltpu.VMEM(member.shape, member.dtype) for member in held]
+        + [
+            pltpu.VMEM((size, width), full),
+            pltpu.VMEM((size, width), low),
+            pltpu.VMEM((size, size), full),
+            pltpu.SemaphoreType.DMA((16,)),
+        ]
+    )
+    operands = [scal, seg_row, code_col, vecs, inc, dffn, dsum, dg, n1, r1, att, qkv, lse, *weights, u, res, *earlier]
+    at_alias = len(operands) - len(earlier)
+    body = partial(chain_kernel, active, len(earlier))
+    return kernel_call(
+        body, outs, scratch, operands, 1, 3, {at_alias + i: i for i in range(len(earlier))}, 10**10, 10**7
+    )
+
+
+def attn_grad_kernel(u_ref, att_ref, dqkv_ref, dbranch_ref, out_ref, flipped):
+    width = u_ref.shape[1]
+    flipped[...] = u_ref[...].T
+
+    def project(at, carry):
+        cols = rows_of(at, 256)
+        out_ref[:, cols] = dot_plain(flipped[...], dqkv_ref[:, cols]).astype(jnp.bfloat16)
+        return carry
+
+    lax.fori_loop(0, 3 * width // 256, project, 0)
+    flipped[...] = att_ref[...].T
+
+    def branch(at, carry):
+        cols = rows_of(at, 256)
+        out_ref[:, rows_of(at + 3 * width // 256, 256)] = dot_plain(flipped[...], dbranch_ref[:, cols]).astype(
+            jnp.bfloat16
+        )
+        return carry
+
+    lax.fori_loop(0, width // 256, branch, 0)
+
+
+def run_attn_grad(u, att, dqkv, dbranch):
+    size, width = u.shape
+    return pl.pallas_call(
+        attn_grad_kernel,
+        out_shape=jax.ShapeDtypeStruct((width, 4 * width), jnp.bfloat16),
+        scratch_shapes=[pltpu.VMEM((width, size), jnp.bfloat16)],
+        cost_estimate=pl.CostEstimate(flops=2 * size * width * 4 * width, bytes_accessed=10**7, transcendentals=0),
+        compiler_params=pltpu.CompilerParams(vmem_limit_bytes=60 * 2**20),
+    )(u, att, dqkv, dbranch)
+
+
+def ffn_grad_kernel(n_pieces, n_blocks, scal, inner_bias_ref, *refs):
+    firsts, dffns = refs[:n_pieces], refs[n_pieces : 2 * n_pieces]
+    win_h, wout_h, out_h = refs[2 * n_pieces : 2 * n_pieces + 3]
+    win, wout, bias, first, dffn, first_t, dffn_t, active, dinner, out, sems = refs[2 * n_pieces + 3 :]
+    width = win.shape[0]
+    each = width // n_blocks
+    size = first.shape[0] // n_pieces
+    own = rows_of(scal[3], width)
+    start = copy_list(
+        [(win_h.at[:, own], win), (wout_h.at[own, :], wout)]
+        + [(piece, first.at[pl.ds(at * size, size)]) for at, piece in enumerate(firsts)]
+        + [(piece, dffn.at[pl.ds(at * size, size)]) for at, piece in enumerate(dffns)],
+        sems,
+    )
+    bias[...] = inner_bias_ref[:, own]
+    for copy in start:
+        copy.wait()
+
+    def tokens(at, carry):
+        rows = rows_of(at, 256)
+        value, grad = first[rows], dffn[rows]
+        first_t[:, rows] = value.T
+        dffn_t[:, rows] = grad.T
+        inner = dot_plain(value, win[...]) + bias[...]
+        active_value, slope = gelu_parts(inner)
+        active[rows] = active_value.astype(jnp.bfloat16)
+        dinner[rows] = (dot_flipped(grad, wout[...]) * slope).astype(jnp.bfloat16)
+        return carry
+
+    lax.fori_loop(0, n_pieces * size // 256, tokens, 0)
+
+    def blocks(at, carry):
+        cols = rows_of(at, 256)
+        inner_part = dot_plain(first_t[...], dinner[:, cols]).astype(jnp.bfloat16)
+        outer_part = dot_plain(dffn_t[...], active[:, cols]).astype(jnp.bfloat16)
+        for block in range(n_blocks):
+            out[2 * each * block : 2 * each * block + each, cols] = inner_part[each * block : each * (block + 1)]
+            out[2 * each * block + each : 2 * each * (block + 1), cols] = outer_part[
+                each * block : each * (block + 1)
+            ]
+        return carry
+
+    lax.fori_loop(0, width // 256, blocks, 0)
+    for copy in copy_list([(out, out_h)], sems, 2 * n_pieces + 2):
+        copy.wait()
+
+
+def run_ffn_grad(scal, inner_bias, firsts, dffns, win, wout, n_blocks):
+    size, width = firsts[0].shape
+    count = len(firsts)
+    low = jnp.bfloat16
+    out = jax.ShapeDtypeStruct((2 * width, width), low)
+    scratch = [
+        pltpu.VMEM((width, width), low),
+        pltpu.VMEM((width, width), low),
+        pltpu.VMEM((1, width), jnp.float32),
+        pltpu.VMEM((count * size, width), low),
+        pltpu.VMEM((count * size, width), low),
+        pltpu.VMEM((width, count * size), low),
+        pltpu.VMEM((width, count * size), low),
+        pltpu.VMEM((count * size, width), low),
+        pltpu.VMEM((count * size, width), low),
+        pltpu.VMEM((2 * width, width), low),
+        pltpu.SemaphoreType.DMA((2 * count + 3,)),
+    ]
+    operands = [scal, inner_bias, *firsts, *dffns, win, wout]
+    return kernel_call(
+        partial(ffn_grad_kernel, count, n_blocks), out, scratch, operands, 1, 1, None, 8 * size * count * width**2, 10**7
+    )
+
+
+def swapped(x, axis, by):
+    return lax.ppermute(x, axis, [(i, i ^ by) for i in range(lax.axis_size(axis))])
+
+
+def swapped_in(section, x, by):
+    length = lax.axis_size("ctx")
+    pairs = [(section * length + i, section * length + (i ^ by)) for i in range(length)]
+    return lax.ppermute(x, ("section", "ctx"), pairs)
+
+
+def pick(x, at, dim=0):
+    return lax.dynamic_index_in_dim(x, at, dim, False)
+
+
+def halved(x, dim, axis, by):
+    own = (lax.axis_index(axis) & by) // by
+    received = swapped(pick(x, 1 - own, dim), axis, by)
+    return (pick(x, own, dim).astype(jnp.float32) + received.astype(jnp.float32)).astype(jnp.bfloat16)
+
+
+def whole_row(pieces, ctx):
+    out = jnp.zeros((len(pieces),) + pieces[0].shape, pieces[0].dtype)
+    for at, piece in enumerate(pieces):
+        out = lax.dynamic_update_index_in_dim(out, piece, ctx ^ at, 0)
+    return out
+
+
+def spread(row_half, ctx):
+    length = lax.axis_size("ctx")
+    size, width = row_half.shape
+    parts = row_half.reshape(length, size // length, width)
+    pieces = [pick(parts, ctx)] + [swapped(pick(parts, ctx ^ k), "ctx", k) for k in range(1, length)]
+    return whole_row(pieces, ctx)
+
+
+def row_body(
+    tokens,
+    segment_ids,
+    padding,
+    dropped,
+    qkv_weight,
+    query_bias,
+    value_bias,
+    attn_weight,
+    attn_bias,
+    attn_gain,
+    attn_shift,
+    inner_weight,
+    inner_bias,
+    outer_weight,
+    outer_bias,
+    ffn_gain,
+    ffn_shift,
+    cotangent,
+):
+    width = tokens.shape[2]
+    half = width // 2
+    length = lax.axis_size("ctx")
+    dp_size = lax.axis_size("dp")
+    section, dp, ctx = (lax.axis_index(name) for name in ("section", "dp", "ctx"))
+    weights = (qkv_weight[0], attn_weight[0], inner_weight[0], outer_weight[0])
+    vecs = jnp.concatenate(
+        [attn_bias, attn_gain, attn_shift, outer_bias, ffn_gain, ffn_shift, query_bias, value_bias]
+    )
+    qkv_bias = jnp.concatenate([query_bias, jnp.zeros_like(query_bias), value_bias], axis=1)
+    qkv_scale = jnp.concatenate(
+        [jnp.full((1, width), HEAD_DIM ** (-0.5), jnp.float32), jnp.ones((1, 2 * width), jnp.float32)], axis=1
+    )
+    small = (qkv_bias, qkv_scale, vecs, inner_bias)
+    scal = jnp.stack([section, ctx, pick(dropped[0], ctx), dp]).astype(jnp.int32)
+
+    ids = jnp.stack([segment_ids, jnp.where(padding == 1, segment_ids, -1)], axis=1)
+    id_pieces = [pick(ids, ctx)] + [swapped(pick(ids, ctx ^ k), "ctx", k) for k in range(1, length)]
+    row_ids = whole_row(id_pieces, ctx)
+    seg_row = row_ids[:, 0].reshape(1, -1)
+    code_col = row_ids[:, 1].reshape(-1, 1)
+    own_tokens = [pick(tokens, ctx)] + [swapped_in(0, pick(tokens, ctx ^ k), k) for k in range(1, length)]
+    own_cot = [pick(cotangent, ctx)] + [swapped_in(1, pick(cotangent, ctx ^ k), k) for k in range(1, length)]
+
+    kept = run_forward(0, scal, seg_row, code_col, small, own_tokens, weights, [])
+    middle = lax.ppermute(kept[10], "section", [(0, 1)])
+    kept = run_forward(1, scal, seg_row, code_col, small, [middle], weights, kept)
+    first = kept[6]
+    firsts = [first] + [swapped(first, "dp", k) for k in range(1, dp_size)]
+    result = kept[10]
+    encoded_half = jnp.where(
+        section == 1, result[:, half:], lax.ppermute(result[:, :half], "section", [(1, 0)])
+    )
+    encoded = spread(encoded_half, ctx)
+
+    top = run_top(1, scal, vecs, own_cot, kept[8], kept[9], [])
+    chain = run_chain(1, scal, seg_row, code_col, vecs, top, kept, weights, [])
+    incoming = lax.ppermute(chain[2], "section", [(1, 0)])
+    top = run_top(0, scal, vecs, [incoming], kept[8], kept[9], top)
+    dffn = top[1]
+    dffns = [dffn] + [swapped(dffn, "dp", k) for k in range(1, dp_size)]
+    chain = run_chain(0, scal, seg_row, code_col, vecs, top, kept, weights, chain)
+    dqkv, dbranch, d_input, chain_vec = chain
+
+    grad_half = jnp.where(section == 0, d_input[:, :half], lax.ppermute(d_input[:, half:], "section", [(0, 1)]))
+    tokens_grad = spread(grad_half, ctx)
+
+    attn_grads = run_attn_grad(kept[0], kept[2], dqkv, dbranch)
+    bits = dp_size.bit_length() - 1
+    blocks = (2,) * bits
+    cut = 2 * width
+    parts = []
+    for number, columns in enumerate((attn_grads[:, :cut], attn_grads[:, cut:])):
+        value = columns.reshape(blocks + (width // dp_size, cut))
+        order = list(range(bits)) if number == 0 else list(reversed(range(bits)))
+        left = list(reversed(range(bits)))
+        for bit in order:
+            value = halved(value, left.index(bit), "dp", 1 << bit)
+            left.remove(bit)
+        parts.append(value)
+    own_rows = jnp.concatenate(parts, axis=1)
+    rows = width // dp_size
+    own_rows = jnp.concatenate(
+        [
+            own_rows[:, : 3 * width].reshape(rows, length, 3 * width // length).transpose(1, 0, 2),
+            own_rows[:, 3 * width :].reshape(rows, length, width // length).transpose(1, 0, 2),
+        ],
+        axis=2,
+    )
+    ffn_grads = run_ffn_grad(scal, inner_bias, firsts, dffns, weights[2], weights[3], length)
+    ffn_rows = ffn_grads.reshape(length, 2 * width // length, width)
+    ctx_bits = length.bit_length() - 1
+
+    def over_ctx(value):
+        value = value.reshape((2,) * ctx_bits + value.shape[1:])
+        left = list(reversed(range(ctx_bits)))
+        for bit in range(ctx_bits):
+            value = halved(value, left.index(bit), "ctx", 1 << bit)
+            left.remove(bit)
+        return value
+
+    own_rows = over_ctx(own_rows).astype(jnp.float32)
+    ffn_rows = over_ctx(ffn_rows)
+    qkv_grad = own_rows[:, : 3 * width // length]
+    attn_grad = own_rows[:, 3 * width // length :]
+    each = width // length
+    inner_grad = lax.ppermute(
+        ffn_rows[:each],
+        ("dp", "ctx"),
+        [(i * length + j, j * length + i) for i in range(dp_size) for j in range(length)],
+    ).astype(jnp.float32)
+    outer_grad = ffn_rows[each:].astype(jnp.float32).T
+
+    vec = jnp.concatenate([top[3], chain_vec])
+    for axis, bound in (("ctx", length), ("dp", dp_size)):
+        by = 1
+        while by < bound:
+            vec = vec + swapped(vec, axis, by)
+            by *= 2
+    return (
+        encoded,
+        tokens_grad,
+        qkv_grad[None],
+        vec[8:9],
+        vec[9:10],
+        attn_grad[None],
+        vec[10:11],
+        vec[11:12],
+        vec[12:13],
+        inner_grad[None],
+        vec[16 : 16 + inner_bias.shape[1] // width].reshape(1, -1),
+        outer_grad[None],
+        vec[0:1],
+        vec[1:2],
+        vec[2:3],
+    )
+
+
 def solution(mesh):
     placed = (
         P("dp", "ctx", None),
@@ -450,8 +1155,14 @@
         P("section", None),
         P("dp", "ctx", None),
     )
+
+    def dispatch(*members):
+        rows = members[0].shape[0]
+        same = rows == lax.axis_size("ctx") == lax.axis_size("dp")
+        return (row_body if same and rows & (rows - 1) == 0 else body)(*members)
+
     return jax.shard_map(
-        body,
+        dispatch,
         mesh=mesh,
         in_specs=placed,
         out_specs=(

time: 1260 us -> 345 us (0.27); the launches traced: 1240 us -> 341 us
  matrix products: 356 us -> 0 us
  blocking collectives: 353 us -> 0 us
  local copies, waits for them, and re-layouts: 239 us -> 23.3 us
  other arithmetic: 148 us -> 12.7 us
  Pallas kernels: 0 us -> 96 us
  starting transfers between devices: 3.06 us -> 54.6 us
  waiting for transfers between devices: 113 us -> 153 us
  between operations: 27.5 us -> 1.47 us
    dot_general x95 -> x0, matrix products: 356 us -> none  [the longest x20 136 us: left_product(): jnp.einsum('ti,to->io', left, right, preferred_element_type=jnp.float32)]
    all_gather x20 -> x0, blocking collectives: 274 us -> none  [the longest x5 94.5 us: layer_forward(): lax.all_gather(key_local, 'ctx', axis=0, tiled=True)]
    ppermute x10 -> x38, waiting for transfers between devices: 5.6 us -> 153 us  [the longest x27 99.3 us: swapped(): lax.ppermute(x, axis, [(i, i ^ by) for i in range(lax.axis_size(axis))])]
    unnamed x683 -> x63, local copies, waits for them, and re-layouts: 114 us -> 5.62 us
    pallas_call x0 -> x8, Pallas kernels: none -> 96 us  [the longest x7 86.6 us: kernel_call(): pl.pallas_call(body, out_shape=out_shapes, in_specs=specs, out_specs=jax....]
    psum x1 -> x0, blocking collectives: 79.7 us -> none  [body(): lax.psum((grad_totals[1][None], grad_totals[2][None], grad_totals[4][None...]
    reduce_sum x50 -> x0, other arithmetic: 70.3 us -> none  [the longest x5 15.1 us: attend_piece(): run_total = jnp.sum(weights, axis=-1)]
    unnamed x31 -> x0, waiting for transfers between devices: 66.6 us -> none
  transfers between devices with their start and end apart: 28 -> 38, of which waited for: 11 -> 18; matrix products, arithmetic and copies ran while one was open for 31% -> 9% of each run, Pallas kernels for 0% -> 20%
where the time goes in v1:
time: 345 us; the launch traced here: 341 us
  waiting for transfers between devices  153 us (44%)
  Pallas kernels  96 us (28%)
  starting transfers between devices  54.6 us (16%)
  local copies, waits for them, and re-layouts  23.3 us (7%)
  other arithmetic  12.7 us (4%)
    ppermute x27, waiting for transfers between devices, swapped(): lax.ppermute(x, axis, [(i, i ^ by) for i in range(lax.axis_size(axis))])  99.3 us
    pallas_call x7, Pallas kernels, kernel_call(): pl.pallas_call(body, out_shape=out_shapes, in_specs=specs, out_specs=jax....  86.6 us
    ppermute x27, starting transfers between devices, swapped(): lax.ppermute(x, axis, [(i, i ^ by) for i in range(lax.axis_size(axis))])  36.3 us
    ppermute x1, waiting for transfers between devices, row_body(): lax.ppermute(result[:, :half], 'section', [(1, 0)])  24.4 us
    ppermute x1, waiting for transfers between devices, row_body(): incoming = lax.ppermute(chain[2], 'section', [(1, 0)])  21 us
    ppermute x6, starting transfers between devices, swapped_in(): return lax.ppermute(x, ('section', 'ctx'), pairs)  12.1 us
    pallas_call x1, Pallas kernels, run_attn_grad(): pl.pallas_call(attn_grad_kernel, out_shape=jax.ShapeDtypeStruct((width, 4...  9.42 us
    ppermute x6, waiting for transfers between devices, swapped_in(): return lax.ppermute(x, ('section', 'ctx'), pairs)  8.05 us
  transfers between devices with their start and end apart: 38, of which 18 were waited for; matrix products, arithmetic and copies ran while one was open for 9% of the time, Pallas kernels for 20%

profile of v1, /device:TPU:0, one launch (start us, length us, event | category | flops | bytes accessed | tf_op | source)
XLA Modules:
  0.0 340.9 jit_solution(15539619680105205271)
XLA Ops:
  2.3 3.1 collective-permute-start
  6.1 2.6 collective-permute-start.1
  8.7 1.9 dynamic-slice_bitcast_fusion.12
  10.6 2.8 collective-permute-start.3
  13.4 5.4 %collective-permute-start.4 = (bf16[128,768]{1,0:T(8,128)(2,1)S(1)}, bf16[128,768]{1,0:T(8,128)(2,1)S(1)}, u32[]{:S(2)}, u32[]{:S(2)}) collective-permute-start(bf16[128,768]{1,0:T(8,128)(2,1)S(1)} %get-tuple-element.100), channel_id=1, source_target_pairs={{0,2},{1,3},{2,0},{3,1},{4,6},{5,7},{6,4},{7,5},{8,10},{9,11},{10,... | collective-permute-start | bytes 589832 | tf_op jit(solution)/shard_map/ppermute | solution.py:971
  20.0 1.3 pad_add_fusion.scal
  22.1 1.9 collective-permute-start.5
  24.7 0.9 copy.61.code_ref
  25.6 8.0 %collective-permute-done.5.refs_3_ = bf16[128,768]{1,0:T(8,128)(2,1)S(1)} collective-permute-done((bf16[128,768]{1,0:T(8,128)(2,1)S(1)}, bf16[128,768]{1,0:T(8,128)(2,1)S(1)}, u32[]{:S(2)}, u32[]{:S(2)}) %collective-permute-start.5) | collective-permute-done | bytes 196640 | tf_op jit(solution)/shard_map/ppermute | solution.py:971
  34.3 29.3 %shard_map.289 = (bf16[512,768]{1,0:T(8,128)(2,1)}, bf16[512,2304]{1,0:T(8,128)(2,1)}, bf16[512,768]{1,0:T(8,128)(2,1)}, f32[16,512]{1,0:T(8,128)}, f32[512,768]...) custom-call(s32[4]{0:T(128)} %pad_add_fusion.scal, ...), custom_call_target="tpu_custom_call" | custom-call | flops 8000000000 | bytes 10000000 | tf_op jit(solution)/shard_map/pallas_call | solution.py:582
  63.7 1.3 collective-permute-start.6
  67.8 0.9 copy-done.26
  68.7 1.1 shard_map.290
  69.8 1.0 slice.72
  70.9 1.3 collective-permute-start.7
  73.9 1.4 shard_map.292
  75.3 1.3 collective-permute-start.14
  76.6 24.4 %collective-permute-done.7 = bf16[512,384]{1,0:T(8,128)(2,1)S(1)} collective-permute-done((bf16[512,384]{1,0:T(8,128)(2,1)S(1)}, bf16[512,384]{1,0:T(8,128)(2,1)S(1)}, u32[]{:S(2)}, u32[]{:S(2)}) %collective-permute-start.7) | collective-permute-done | bytes 393248 | tf_op jit(solution)/shard_map/ppermute | solution.py:1050
  101.3 1.6 collective-permute-start.29
  102.9 1.5 collective-permute-start.30
  104.9 1.0 collective-permute-done.8
  105.9 2.9 collective-permute-start.9
  108.8 3.7 %collective-permute-done.9 = bf16[128,384]{1,0:T(8,128)(2,1)S(1)} collective-permute-done((bf16[128,384]{1,0:T(8,128)(2,1)S(1)}, bf16[128,384]{1,0:T(8,128)(2,1)S(1)}, u32[]{:S(2)}, u32[]{:S(2)}) %collective-permute-start.9) | collective-permute-done | bytes 98336 | tf_op jit(solution)/shard_map/ppermute | solution.py:965
  112.4 3.2 collective-permute-start.10
  115.7 3.2 collective-permute-done.10
  118.9 21.0 %collective-permute-done.14.refs_0_ = bf16[512,768]{1,0:T(8,128)(2,1)S(1)} collective-permute-done((bf16[512,768]{1,0:T(8,128)(2,1)}, bf16[512,768]{1,0:T(8,128)(2,1)S(1)}, u32[]{:S(2)}, u32[]{:S(2)}) %collective-permute-start.14) | collective-permute-done | bytes 786464 | tf_op jit(solution)/shard_map/ppermute | solution.py:1056
  139.9 0.9 copy-done.7
  140.8 5.8 %shard_map.293 = (bf16[512,768]{1,0:T(8,128)(2,1)}, bf16[512,768]{1,0:T(8,128)(2,1)}, f32[512,768]{1,0:T(8,128)}, f32[8,768]{1,0:T(8,128)}) custom-call(s32[4]{0:T(128)} %pad_add_fusion.scal, f32[8,768]{1,0:T(8,128)} %concatenate.16.vec_ref, bf16[512,768]{1,0:T(8,128)(2,1)} %copy-done.7, ...), custom_call_target="tpu_custom_call", output_to_operand_aliasing={{0}: (5, {}), {1}: (6, {}), {2}: (7, {}), {3}: (8, {})} | custom-call | flops 10000000 | bytes 10000000 | tf_op jit(solution)/shard_map/pallas_call | solution.py:582
  147.3 29.8 %shard_map.294 = (bf16[512,2304]{1,0:T(8,128)(2,1)}, bf16[512,768]{1,0:T(8,128)(2,1)}, bf16[512,768]{1,0:T(8,128)(2,1)}, f32[16,768]{1,0:T(8,128)}) custom-call(s32[4]{0:T(128)} %pad_add_fusion.scal, s32[1,512]{1,0:T(1,128)} %bitcast.145, s32[512,1]{1,0:T(8,128)} %copy.61.code_ref, ...), custom_call_target="tpu_custom_call", output_to_operand_aliasing={{0}: (19, {}), {1}: (20, {}), {2}: (21, {}), {3}: (22, {})} | custom-call | flops 10000000000 | bytes 10000000 | tf_op jit(solution)/shard_map/pallas_call | solution.py:582
  177.9 9.4 %shard_map.295 = bf16[768,3072]{1,0:T(8,128)(2,1)} custom-call(bf16[512,768]{1,0:T(8,128)(2,1)} %get-tuple-element.76.refs_13_.u_ref, bf16[512,768]{1,0:T(8,128)(2,1)} %get-tuple-element.73.refs_6_.att_ref, bf16[512,2304]{1,0:T(8,128)(2,1)} %get-tuple-element.86.dqkv_ref, bf16[512,768]{1,0:T(8,128)(2,1)} %get-tuple-element.87.dbranch_ref), custom_call_target="tpu_custom_call" | custom-call | flops 2415919104 | bytes 10000000 | tf_op jit(solution)/shard_map/pallas_call | solution.py:884
  187.3 3.0 collective-permute-start.26
  190.3 2.7 fusion.14
  193.0 1.5 collective-permute-start.15
  194.6 1.6 collective-permute-start.27
  196.3 2.8 collective-permute-done.27
  199.0 1.6 collective-permute-start.28
  200.6 1.2 dynamic-slice_bitcast_fusion.1
  201.8 9.4 %collective-permute-done.28 = f32[24,768]{1,0:T(8,128)S(1)} collective-permute-done((f32[24,768]{1,0:T(8,128)S(1)}, f32[24,768]{1,0:T(8,128)S(1)}, u32[]{:S(2)}, u32[]{:S(2)}) %collective-permute-start.28) | collective-permute-done | bytes 73760 | tf_op jit(solution)/shard_map/ppermute | solution.py:965
  211.2 1.5 collective-permute-start.32
  213.5 1.5 collective-permute-start.34
  215.0 2.0 collective-permute-start.16
  217.7 2.0 collective-permute-done.16
  220.4 4.8 %collective-permute-done.17 = bf16[128,384]{1,0:T(8,128)(2,1)S(1)} collective-permute-done((bf16[128,384]{1,0:T(8,128)(2,1)S(1)}, bf16[128,384]{1,0:T(8,128)(2,1)S(1)}, u32[]{:S(2)}, u32[]{:S(2)}) %collective-permute-start.17) | collective-permute-done | bytes 98336 | tf_op jit(solution)/shard_map/ppermute | solution.py:965
  225.7 1.6 collective-permute-start.19
  227.3 4.4 %collective-permute-done.32.refs_5_ = bf16[512,768]{1,0:T(8,128)(2,1)S(1)} collective-permute-done((bf16[512,768]{1,0:T(8,128)(2,1)S(1)}, bf16[512,768]{1,0:T(8,128)(2,1)S(1)}, u32[]{:S(2)}, u32[]{:S(2)}) %collective-permute-start.32) | collective-permute-done | bytes 786464 | tf_op jit(solution)/shard_map/ppermute | solution.py:965
  231.7 1.6 collective-permute-start.18
  233.2 8.4 %collective-permute-done.33.refs_6_ = bf16[512,768]{1,0:T(8,128)(2,1)S(1)} collective-permute-done((bf16[512,768]{1,0:T(8,128)(2,1)S(1)}, bf16[512,768]{1,0:T(8,128)(2,1)S(1)}, u32[]{:S(2)}, u32[]{:S(2)}) %collective-permute-start.33) | collective-permute-done | bytes 786464 | tf_op jit(solution)/shard_map/ppermute | solution.py:965
  241.7 0.9 copy-done.25
  242.6 18.4 %shard_map.296 = bf16[1536,768]{1,0:T(8,128)(2,1)} custom-call(s32[4]{0:T(128)} %pad_add_fusion.scal, f32[1,3072]{1,0:T(1,128)} %inner_bias_ref.5, bf16[512,768]{1,0:T(8,128)(2,1)} %get-tuple-element.90.refs_0_, bf16[512,768]{1,0:T(8,128)(2,1)} %collective-permute-done.29.refs_1_, bf16[512,768]{1,0:T(8,128)(2,1)} %collective-permute-done.30.refs_2_, ...), custom_call_target="tpu_custom_call" | custom-call | flops 9663676416 | bytes 10000000 | tf_op jit(solution)/shard_map/pallas_call | solution.py:582
  261.0 1.9 fusion.1
  263.6 1.8 fusion.2
  266.0 1.1 dynamic-slice_bitcast_fusion
  267.1 2.0 collective-permute-start.35
  269.1 3.8 %collective-permute-done.22 = bf16[192,1536]{1,0:T(8,128)(2,1)S(1)} collective-permute-done((bf16[192,1536]{1,0:T(8,128)(2,1)S(1)}, bf16[192,1536]{1,0:T(8,128)(2,1)S(1)}, u32[]{:S(2)}, u32[]{:S(2)}) %collective-permute-start.22) | collective-permute-done | bytes 589856 | tf_op jit(solution)/shard_map/ppermute | solution.py:965
  273.0 2.3 collective-permute-done.20
  275.6 1.1 reshape.75
  278.1 2.1 collective-permute-start.23
  280.2 20.5 %collective-permute-done.35 = bf16[2,384,768]{2,1,0:T(8,128)(2,1)} collective-permute-done((bf16[2,384,768]{2,1,0:T(8,128)(2,1)}, bf16[2,384,768]{2,1,0:T(8,128)(2,1)}, u32[]{:S(2)}, u32[]{:S(2)}) %collective-permute-start.35) | collective-permute-done | bytes 1179680 | tf_op jit(solution)/shard_map/ppermute | solution.py:965
  300.6 1.6 fusion
  302.3 0.9 bitcast_dynamic-update-slice_fusion
  303.3 8.0 %collective-permute-done.23 = bf16[2,192,768]{2,1,0:T(8,128)(2,1)S(1)} collective-permute-done((bf16[2,192,768]{2,1,0:T(8,128)(2,1)S(1)}, bf16[2,192,768]{2,1,0:T(8,128)(2,1)S(1)}, u32[]{:S(2)}, u32[]{:S(2)}) %collective-permute-start.23) | collective-permute-done | bytes 589856 | tf_op jit(solution)/shard_map/ppermute | solution.py:965
  311.6 20.3 %collective-permute-done.36 = bf16[384,768]{1,0:T(8,128)(2,1)S(1)} collective-permute-done((bf16[384,768]{1,0:T(8,128)(2,1)S(1)}, bf16[384,768]{1,0:T(8,128)(2,1)S(1)}, u32[]{:S(2)}, u32[]{:S(2)}) %collective-permute-start.36) | collective-permute-done | bytes 589856 | tf_op jit(solution)/shard_map/ppermute | solution.py:965
  332.1 0.9 convert_bitcast_fusion
  333.6 4.7 %collective-permute-done.24 = bf16[192,768]{1,0:T(8,128)(2,1)S(1)} collective-permute-done((bf16[192,768]{1,0:T(8,128)(2,1)S(1)}, bf16[192,768]{1,0:T(8,128)(2,1)S(1)}, u32[]{:S(2)}, u32[]{:S(2)}) %collective-permute-start.24) | collective-permute-done | bytes 294944 | tf_op jit(solution)/shard_map/ppermute | solution.py:965
  (149 shorter events, 21.8 us)
Async XLA Ops:
  0.7 18.2 %copy-start = (s32[1,4]{1,0:T(1,128)S(1)}, s32[1,4]{1,0:T(1,128)}, u32[]{:S(2)}) copy-start(s32[1,4]{1,0:T(1,128)} %param.21) | copy-start | bytes 52
  0.7 18.8 %copy-start.17 = (f32[1,768]{1,0:T(1,128)S(1)}, f32[1,768]{1,0:T(1,128)}, u32[]{:S(2)}) copy-start(f32[1,768]{1,0:T(1,128)} %param.23) | copy-start | bytes 9220
  0.7 18.8 %copy-start.16 = (f32[1,768]{1,0:T(1,128)S(1)}, f32[1,768]{1,0:T(1,128)}, u32[]{:S(2)}) copy-start(f32[1,768]{1,0:T(1,128)} %param.24) | copy-start | bytes 9220
  0.7 20.7 %copy-start.18 = (f32[1,768]{1,0:T(1,128)S(1)}, f32[1,768]{1,0:T(1,128)}, u32[]{:S(2)}) copy-start(f32[1,768]{1,0:T(1,128)} %param.26) | copy-start | bytes 9220
  0.7 20.7 %copy-start.19 = (f32[1,768]{1,0:T(1,128)S(1)}, f32[1,768]{1,0:T(1,128)}, u32[]{:S(2)}) copy-start(f32[1,768]{1,0:T(1,128)} %param.27) | copy-start | bytes 9220
  0.7 20.7 %copy-start.20 = (f32[1,768]{1,0:T(1,128)S(1)}, f32[1,768]{1,0:T(1,128)}, u32[]{:S(2)}) copy-start(f32[1,768]{1,0:T(1,128)} %param.28) | copy-start | bytes 9220
  0.7 20.7 %copy-start.21 = (f32[1,768]{1,0:T(1,128)S(1)}, f32[1,768]{1,0:T(1,128)}, u32[]{:S(2)}) copy-start(f32[1,768]{1,0:T(1,128)} %param.32) | copy-start | bytes 9220
  0.7 20.7 %copy-start.22 = (f32[1,768]{1,0:T(1,128)S(1)}, f32[1,768]{1,0:T(1,128)}, u32[]{:S(2)}) copy-start(f32[1,768]{1,0:T(1,128)} %param.33) | copy-start | bytes 9220
  0.7 20.7 %copy-start.23 = (f32[1,768]{1,0:T(1,128)S(1)}, f32[1,768]{1,0:T(1,128)}, u32[]{:S(2)}) copy-start(f32[1,768]{1,0:T(1,128)} %param.34) | copy-start | bytes 9220
  2.3 19.8 %collective-permute-start = (s32[2,128]{1,0:T(2,128)S(1)}, s32[2,128]{1,0:T(2,128)S(1)}, u32[]{:S(2)}, u32[]{:S(2)}) collective-permute-start(s32[2,128]{1,0:T(2,128)S(1)} %bitcast.148), channel_id=1, source_target_pairs={{0,1},{1,0},{2,3},{3,2},{4,5},{5,4},{6,7},{7,6},{8,9},{9,8},{10,11... | collective-permute-start | bytes 3080 | tf_op jit(solution)/shard_map/ppermute | solution.py:965
  6.1 18.0 %collective-permute-start.1 = (s32[2,128]{1,0:T(2,128)S(1)}, s32[2,128]{1,0:T(2,128)S(1)}, u32[]{:S(2)}, u32[]{:S(2)}) collective-permute-start(s32[2,128]{1,0:T(2,128)S(1)} %bitcast.151), channel_id=1, source_target_pairs={{0,2},{1,3},{2,0},{3,1},{4,6},{5,7},{6,4},{7,5},{8,10},{9,11},{10,... | collective-permute-start | bytes 3080 | tf_op jit(solution)/shard_map/ppermute | solution.py:965
  8.7 15.4 %collective-permute-start.2 = (s32[2,128]{1,0:T(2,128)S(1)}, s32[2,128]{1,0:T(2,128)S(1)}, u32[]{:S(2)}, u32[]{:S(2)}) collective-permute-start(s32[2,128]{1,0:T(2,128)S(1)} %bitcast.146), channel_id=1, source_target_pairs={{0,3},{1,2},{2,1},{3,0},{4,7},{5,6},{6,5},{7,4},{8,11},{9,10},{10,... | collective-permute-start | bytes 3080 | tf_op jit(solution)/shard_map/ppermute | solution.py:965
  10.6 15.0 %collective-permute-start.3 = (bf16[128,768]{1,0:T(8,128)(2,1)S(1)}, bf16[128,768]{1,0:T(8,128)(2,1)S(1)}, u32[]{:S(2)}, u32[]{:S(2)}) collective-permute-start(bf16[128,768]{1,0:T(8,128)(2,1)S(1)} %get-tuple-element.98), channel_id=1, source_target_pairs={{0,1},{1,0},{2,3},{3,2},{4,5},{5,4},{6,7},{7,6},{8,9},{9,8},{10,11... | collective-permute-start | bytes 589832 | tf_op jit(solution)/shard_map/ppermute | solution.py:971
  13.4 12.2 %collective-permute-start.4 = (bf16[128,768]{1,0:T(8,128)(2,1)S(1)}, bf16[128,768]{1,0:T(8,128)(2,1)S(1)}, u32[]{:S(2)}, u32[]{:S(2)}) collective-permute-start(bf16[128,768]{1,0:T(8,128)(2,1)S(1)} %get-tuple-element.100), channel_id=1, source_target_pairs={{0,2},{1,3},{2,0},{3,1},{4,6},{5,7},{6,4},{7,5},{8,10},{9,11},{10,... | collective-permute-start | bytes 589832 | tf_op jit(solution)/shard_map/ppermute | solution.py:971
  22.1 11.5 %collective-permute-start.5 = (bf16[128,768]{1,0:T(8,128)(2,1)S(1)}, bf16[128,768]{1,0:T(8,128)(2,1)S(1)}, u32[]{:S(2)}, u32[]{:S(2)}) collective-permute-start(bf16[128,768]{1,0:T(8,128)(2,1)S(1)} %get-tuple-element.97), channel_id=1, source_target_pairs={{0,3},{1,2},{2,1},{3,0},{4,7},{5,6},{6,5},{7,4},{8,11},{9,10},{10,... | collective-permute-start | bytes 589832 | tf_op jit(solution)/shard_map/ppermute | solution.py:971
  25.6 8.1 %copy-start.27 = (bf16[128,768]{1,0:T(8,128)(2,1)}, bf16[128,768]{1,0:T(8,128)(2,1)S(1)}, u32[]{:S(2)}) copy-start(bf16[128,768]{1,0:T(8,128)(2,1)S(1)} %collective-permute-done.3.refs_1_) | copy-start | bytes 589828
  25.6 8.1 %copy-start.28 = (bf16[128,768]{1,0:T(8,128)(2,1)}, bf16[128,768]{1,0:T(8,128)(2,1)S(1)}, u32[]{:S(2)}) copy-start(bf16[128,768]{1,0:T(8,128)(2,1)S(1)} %collective-permute-done.4.refs_2_) | copy-start | bytes 589828
  34.3 30.7 %copy-start.8 = (bf16[4,128,768]{2,1,0:T(8,128)(2,1)S(1)}, bf16[4,128,768]{2,1,0:T(8,128)(2,1)}, u32[]{:S(2)}) copy-start(bf16[4,128,768]{2,1,0:T(8,128)(2,1)} %param.35) | copy-start | bytes 2359300
  63.7 4.1 %collective-permute-start.6 = (bf16[512,768]{1,0:T(8,128)(2,1)}, bf16[512,768]{1,0:T(8,128)(2,1)S(1)}, u32[]{:S(2)}, u32[]{:S(2)}) collective-permute-start(bf16[512,768]{1,0:T(8,128)(2,1)} %get-tuple-element.53.refs_15_), channel_id=1, source_target_pairs={{0,16},{1,17},{2,18},{3,19},{4,20},{5,21},{6,22},{7,23},{8,24},{9,... | collective-permute-start | bytes 2359304 | tf_op jit(solution)/shard_map/ppermute | solution.py:1044
  65.8 6.4 %collective-permute-start.11 = (bf16[128,768]{1,0:T(8,128)(2,1)S(1)}, bf16[128,768]{1,0:T(8,128)(2,1)S(1)}, u32[]{:S(2)}, u32[]{:S(2)}) collective-permute-start(bf16[128,768]{1,0:T(8,128)(2,1)S(1)} %get-tuple-element.94), channel_id=1, source_target_pairs={{16,17},{17,16},{18,19},{19,18},{20,21},{21,20},{22,23},{23,22},{2... | collective-permute-start | bytes 589832 | tf_op jit(solution)/shard_map/ppermute | solution.py:971
  66.4 5.8 %collective-permute-start.12 = (bf16[128,768]{1,0:T(8,128)(2,1)S(1)}, bf16[128,768]{1,0:T(8,128)(2,1)S(1)}, u32[]{:S(2)}, u32[]{:S(2)}) collective-permute-start(bf16[128,768]{1,0:T(8,128)(2,1)S(1)} %get-tuple-element.96), channel_id=1, source_target_pairs={{16,18},{17,19},{18,16},{19,17},{20,22},{21,23},{22,20},{23,21},{2... | collective-permute-start | bytes 589832 | tf_op jit(solution)/shard_map/ppermute | solution.py:971
  67.1 5.1 %collective-permute-start.13 = (bf16[128,768]{1,0:T(8,128)(2,1)S(1)}, bf16[128,768]{1,0:T(8,128)(2,1)S(1)}, u32[]{:S(2)}, u32[]{:S(2)}) collective-permute-start(bf16[128,768]{1,0:T(8,128)(2,1)S(1)} %get-tuple-element.93), channel_id=1, source_target_pairs={{16,19},{17,18},{18,17},{19,16},{20,23},{21,22},{22,21},{23,20},{2... | collective-permute-start | bytes 589832 | tf_op jit(solution)/shard_map/ppermute | solution.py:971
  67.8 0.9 copy-start.26
  70.9 30.1 %collective-permute-start.7 = (bf16[512,384]{1,0:T(8,128)(2,1)S(1)}, bf16[512,384]{1,0:T(8,128)(2,1)S(1)}, u32[]{:S(2)}, u32[]{:S(2)}) collective-permute-start(bf16[512,384]{1,0:T(8,128)(2,1)S(1)} %slice.72), channel_id=1, source_target_pairs={{16,0},{17,1},{18,2},{19,3},{20,4},{21,5},{22,6},{23,7},{24,8},{25... | collective-permute-start | bytes 1179656 | tf_op jit(solution)/shard_map/ppermute | solution.py:1050
  73.9 27.1 %copy-start.10 = (bf16[512,768]{1,0:T(8,128)(2,1)S(1)}, bf16[512,768]{1,0:T(8,128)(2,1)}, u32[]{:S(2)}) copy-start(bf16[512,768]{1,0:T(8,128)(2,1)} %get-tuple-element.64.refs_14_) | copy-start | bytes 2359300
  75.3 64.6 %collective-permute-start.14 = (bf16[512,768]{1,0:T(8,128)(2,1)}, bf16[512,768]{1,0:T(8,128)(2,1)S(1)}, u32[]{:S(2)}, u32[]{:S(2)}) collective-permute-start(bf16[512,768]{1,0:T(8,128)(2,1)} %get-tuple-element.77.refs_17_), channel_id=1, source_target_pairs={{16,0},{17,1},{18,2},{19,3},{20,4},{21,5},{22,6},{23,7},{24,8},{25... | collective-permute-start | bytes 2359304 | tf_op jit(solution)/shard_map/ppermute | solution.py:1056
  101.2 4.7 %collective-permute-start.8 = (bf16[128,384]{1,0:T(8,128)(2,1)S(1)}, bf16[128,384]{1,0:T(8,128)(2,1)S(1)}, u32[]{:S(2)}, u32[]{:S(2)}) collective-permute-start(bf16[128,384]{1,0:T(8,128)(2,1)S(1)} %get-tuple-element.109), channel_id=1, source_target_pairs={{0,1},{1,0},{2,3},{3,2},{4,5},{5,4},{6,7},{7,6},{8,9},{9,8},{10,11... | collective-permute-start | bytes 294920 | tf_op jit(solution)/shard_map/ppermute | solution.py:965
  101.3 112.2 %collective-permute-start.29 = (bf16[512,768]{1,0:T(8,128)(2,1)}, bf16[512,768]{1,0:T(8,128)(2,1)}, u32[]{:S(2)}, u32[]{:S(2)}) collective-permute-start(bf16[512,768]{1,0:T(8,128)(2,1)} %get-tuple-element.90.refs_0_), channel_id=1, source_target_pairs={{0,4},{4,0},{8,12},{12,8},{1,5},{5,1},{9,13},{13,9},{2,6},{6,2},{1... | collective-permute-start | bytes 2359304 | tf_op jit(solution)/shard_map/ppermute | solution.py:965
  102.9 112.2 %collective-permute-start.30 = (bf16[512,768]{1,0:T(8,128)(2,1)}, bf16[512,768]{1,0:T(8,128)(2,1)}, u32[]{:S(2)}, u32[]{:S(2)}) collective-permute-start(bf16[512,768]{1,0:T(8,128)(2,1)} %get-tuple-element.90.refs_0_), channel_id=1, source_target_pairs={{0,8},{4,12},{8,0},{12,4},{1,9},{5,13},{9,1},{13,5},{2,10},{6,14},... | collective-permute-start | bytes 2359304 | tf_op jit(solution)/shard_map/ppermute | solution.py:965
  104.4 121.3 %collective-permute-start.31 = (bf16[512,768]{1,0:T(8,128)(2,1)}, bf16[512,768]{1,0:T(8,128)(2,1)}, u32[]{:S(2)}, u32[]{:S(2)}) collective-permute-start(bf16[512,768]{1,0:T(8,128)(2,1)} %get-tuple-element.90.refs_0_), channel_id=1, source_target_pairs={{0,12},{4,8},{8,4},{12,0},{1,13},{5,9},{9,5},{13,1},{2,14},{6,10},... | collective-permute-start | bytes 2359304 | tf_op jit(solution)/shard_map/ppermute | solution.py:965
  105.9 6.6 %collective-permute-start.9 = (bf16[128,384]{1,0:T(8,128)(2,1)S(1)}, bf16[128,384]{1,0:T(8,128)(2,1)S(1)}, u32[]{:S(2)}, u32[]{:S(2)}) collective-permute-start(bf16[128,384]{1,0:T(8,128)(2,1)S(1)} %get-tuple-element.108), channel_id=1, source_target_pairs={{0,2},{1,3},{2,0},{3,1},{4,6},{5,7},{6,4},{7,5},{8,10},{9,11},{10,... | collective-permute-start | bytes 294920 | tf_op jit(solution)/shard_map/ppermute | solution.py:965
  112.4 6.4 %collective-permute-start.10 = (bf16[128,384]{1,0:T(8,128)(2,1)S(1)}, bf16[128,384]{1,0:T(8,128)(2,1)S(1)}, u32[]{:S(2)}, u32[]{:S(2)}) collective-permute-start(bf16[128,384]{1,0:T(8,128)(2,1)S(1)} %get-tuple-element.107), channel_id=1, source_target_pairs={{0,3},{1,2},{2,1},{3,0},{4,7},{5,6},{6,5},{7,4},{8,11},{9,10},{10,... | collective-permute-start | bytes 294920 | tf_op jit(solution)/shard_map/ppermute | solution.py:965
  118.9 58.2 %copy-start.12 = (bf16[4,128,384]{2,1,0:T(8,128)(2,1)}, bf16[4,128,384]{2,1,0:T(8,128)(2,1)S(1)}, u32[]{:S(2)}) copy-start(bf16[4,128,384]{2,1,0:T(8,128)(2,1)S(1)} %bitcast_dynamic-update-slice_fusion.3) | copy-start | bytes 1179652
  139.9 0.9 copy-start.7
  177.9 9.4 %collective-permute-start.25 = (f32[24,768]{1,0:T(8,128)S(1)}, f32[24,768]{1,0:T(8,128)S(1)}, u32[]{:S(2)}, u32[]{:S(2)}) collective-permute-start(f32[24,768]{1,0:T(8,128)S(1)} %constant_dynamic-update-slice_fusion), channel_id=1, source_target_pairs={{0,1},{1,0},{2,3},{3,2},{4,5},{5,4},{6,7},{7,6},{8,9},{9,8},{10,11... | collective-permute-start | bytes 221192 | tf_op jit(solution)/shard_map/ppermute | solution.py:965
  187.3 5.7 %copy-start.9 = (bf16[512,768]{1,0:T(8,128)(2,1)S(1)}, bf16[512,768]{1,0:T(8,128)(2,1)}, u32[]{:S(2)}) copy-start(bf16[512,768]{1,0:T(8,128)(2,1)} %get-tuple-element.85) | copy-start | bytes 2359300
  187.3 7.3 %collective-permute-start.26 = (f32[24,768]{1,0:T(8,128)S(1)}, f32[24,768]{1,0:T(8,128)S(1)}, u32[]{:S(2)}, u32[]{:S(2)}) collective-permute-start(f32[24,768]{1,0:T(8,128)S(1)} %add.148), channel_id=1, source_target_pairs={{0,2},{1,3},{2,0},{3,1},{4,6},{5,7},{6,4},{7,5},{8,10},{9,11},{10,... | collective-permute-start | bytes 221192 | tf_op jit(solution)/shard_map/ppermute | solution.py:965
  193.0 7.7 %copy-start.2 = (bf16[768,1536]{1,0:T(8,128)(2,1)}, bf16[768,1536]{1,0:T(8,128)(2,1)S(1)}, u32[]{:S(2)}) copy-start(bf16[768,1536]{1,0:T(8,128)(2,1)S(1)} %get-tuple-element.92) | copy-start | bytes 7077892
  193.0 19.7 %collective-permute-start.15 = (bf16[512,384]{1,0:T(8,128)(2,1)S(1)}, bf16[512,384]{1,0:T(8,128)(2,1)S(1)}, u32[]{:S(2)}, u32[]{:S(2)}) collective-permute-start(bf16[512,384]{1,0:T(8,128)(2,1)S(1)} %slice.74), channel_id=1, source_target_pairs={{0,16},{1,17},{2,18},{3,19},{4,20},{5,21},{6,22},{7,23},{8,24},{9,... | collective-permute-start | bytes 1179656 | tf_op jit(solution)/shard_map/ppermute | solution.py:1063
  194.6 4.4 %collective-permute-start.27 = (f32[24,768]{1,0:T(8,128)S(1)}, f32[24,768]{1,0:T(8,128)S(1)}, u32[]{:S(2)}, u32[]{:S(2)}) collective-permute-start(f32[24,768]{1,0:T(8,128)S(1)} %add.149), channel_id=1, source_target_pairs={{0,4},{4,0},{8,12},{12,8},{1,5},{5,1},{9,13},{13,9},{2,6},{6,2},{1... | collective-permute-start | bytes 221192 | tf_op jit(solution)/shard_map/ppermute | solution.py:965
  199.0 12.1 %collective-permute-start.28 = (f32[24,768]{1,0:T(8,128)S(1)}, f32[24,768]{1,0:T(8,128)S(1)}, u32[]{:S(2)}, u32[]{:S(2)}) collective-permute-start(f32[24,768]{1,0:T(8,128)S(1)} %add.150), channel_id=1, source_target_pairs={{0,8},{4,12},{8,0},{12,4},{1,9},{5,13},{9,1},{13,5},{2,10},{6,14},... | collective-permute-start | bytes 221192 | tf_op jit(solution)/shard_map/ppermute | solution.py:965
  200.6 10.6 %copy-start.6 = (bf16[512,768]{1,0:T(8,128)(2,1)S(1)}, bf16[512,768]{1,0:T(8,128)(2,1)}, u32[]{:S(2)}) copy-start(bf16[512,768]{1,0:T(8,128)(2,1)} %get-tuple-element.80.refs_1_.refs_4_) | copy-start | bytes 2359300
  211.2 20.5 %collective-permute-start.32 = (bf16[512,768]{1,0:T(8,128)(2,1)S(1)}, bf16[512,768]{1,0:T(8,128)(2,1)S(1)}, u32[]{:S(2)}, u32[]{:S(2)}) collective-permute-start(bf16[512,768]{1,0:T(8,128)(2,1)S(1)} %copy-done.6), channel_id=1, source_target_pairs={{0,4},{4,0},{8,12},{12,8},{1,5},{5,1},{9,13},{13,9},{2,6},{6,2},{1... | collective-permute-start | bytes 2359304 | tf_op jit(solution)/shard_map/ppermute | solution.py:965
  212.7 29.0 %collective-permute-start.33 = (bf16[512,768]{1,0:T(8,128)(2,1)S(1)}, bf16[512,768]{1,0:T(8,128)(2,1)S(1)}, u32[]{:S(2)}, u32[]{:S(2)}) collective-permute-start(bf16[512,768]{1,0:T(8,128)(2,1)S(1)} %copy-done.6), channel_id=1, source_target_pairs={{0,8},{4,12},{8,0},{12,4},{1,9},{5,13},{9,1},{13,5},{2,10},{6,14},... | collective-permute-start | bytes 2359304 | tf_op jit(solution)/shard_map/ppermute | solution.py:965
  213.5 29.1 %collective-permute-start.34 = (bf16[512,768]{1,0:T(8,128)(2,1)S(1)}, bf16[512,768]{1,0:T(8,128)(2,1)}, u32[]{:S(2)}, u32[]{:S(2)}) collective-permute-start(bf16[512,768]{1,0:T(8,128)(2,1)S(1)} %copy-done.6), channel_id=1, source_target_pairs={{0,12},{4,8},{8,4},{12,0},{1,13},{5,9},{9,5},{13,1},{2,14},{6,10},... | collective-permute-start | bytes 2359304 | tf_op jit(solution)/shard_map/ppermute | solution.py:965
  215.0 4.6 %collective-permute-start.16 = (bf16[128,384]{1,0:T(8,128)(2,1)S(1)}, bf16[128,384]{1,0:T(8,128)(2,1)S(1)}, u32[]{:S(2)}, u32[]{:S(2)}) collective-permute-start(bf16[128,384]{1,0:T(8,128)(2,1)S(1)} %get-tuple-element.105), channel_id=1, source_target_pairs={{0,1},{1,0},{2,3},{3,2},{4,5},{5,4},{6,7},{7,6},{8,9},{9,8},{10,11... | collective-permute-start | bytes 294920 | tf_op jit(solution)/shard_map/ppermute | solution.py:965
  219.6 5.5 %collective-permute-start.17 = (bf16[128,384]{1,0:T(8,128)(2,1)S(1)}, bf16[128,384]{1,0:T(8,128)(2,1)S(1)}, u32[]{:S(2)}, u32[]{:S(2)}) collective-permute-start(bf16[128,384]{1,0:T(8,128)(2,1)S(1)} %get-tuple-element.104), channel_id=1, source_target_pairs={{0,2},{1,3},{2,0},{3,1},{4,6},{5,7},{6,4},{7,5},{8,10},{9,11},{10,... | collective-permute-start | bytes 294920 | tf_op jit(solution)/shard_map/ppermute | solution.py:965
  225.2 35.8 %collective-permute-start.21 = (bf16[2,192,1536]{2,1,0:T(8,128)(2,1)}, bf16[2,192,1536]{2,1,0:T(8,128)(2,1)}, u32[]{:S(2)}, u32[]{:S(2)}) collective-permute-start(bf16[2,192,1536]{2,1,0:T(8,128)(2,1)} %dynamic-slice_bitcast_fusion.1), channel_id=1, source_target_pairs={{0,8},{4,12},{8,0},{12,4},{1,9},{5,13},{9,1},{13,5},{2,10},{6,14},... | collective-permute-start | bytes 3538952 | tf_op jit(solution)/shard_map/ppermute | solution.py:965
  225.7 37.8 %collective-permute-start.19 = (bf16[2,192,1536]{2,1,0:T(8,128)(2,1)S(1)}, bf16[2,192,1536]{2,1,0:T(8,128)(2,1)}, u32[]{:S(2)}, u32[]{:S(2)}) collective-permute-start(bf16[2,192,1536]{2,1,0:T(8,128)(2,1)S(1)} %dynamic-slice_bitcast_fusion.2), channel_id=1, source_target_pairs={{0,4},{4,0},{8,12},{12,8},{1,5},{5,1},{9,13},{13,9},{2,6},{6,2},{1... | collective-permute-start | bytes 3538952 | tf_op jit(solution)/shard_map/ppermute | solution.py:965
  231.7 10.0 %copy-start.24 = (bf16[512,768]{1,0:T(8,128)(2,1)}, bf16[512,768]{1,0:T(8,128)(2,1)S(1)}, u32[]{:S(2)}) copy-start(bf16[512,768]{1,0:T(8,128)(2,1)S(1)} %collective-permute-done.32.refs_5_) | copy-start | bytes 2359300
  231.7 70.7 %collective-permute-start.18 = (bf16[128,384]{1,0:T(8,128)(2,1)S(1)}, bf16[128,384]{1,0:T(8,128)(2,1)}, u32[]{:S(2)}, u32[]{:S(2)}) collective-permute-start(bf16[128,384]{1,0:T(8,128)(2,1)S(1)} %get-tuple-element.103), channel_id=1, source_target_pairs={{0,3},{1,2},{2,1},{3,0},{4,7},{5,6},{6,5},{7,4},{8,11},{9,10},{10,... | collective-permute-start | bytes 294920 | tf_op jit(solution)/shard_map/ppermute | solution.py:965
  262.9 9.9 %collective-permute-start.22 = (bf16[192,1536]{1,0:T(8,128)(2,1)S(1)}, bf16[192,1536]{1,0:T(8,128)(2,1)S(1)}, u32[]{:S(2)}, u32[]{:S(2)}) collective-permute-start(bf16[192,1536]{1,0:T(8,128)(2,1)S(1)} %dynamic-slice_bitcast_fusion.5), channel_id=1, source_target_pairs={{0,4},{4,0},{8,12},{12,8},{1,5},{5,1},{9,13},{13,9},{2,6},{6,2},{1... | collective-permute-start | bytes 1769480 | tf_op jit(solution)/shard_map/ppermute | solution.py:965
  263.6 2.4 copy-start.4
  265.4 9.9 %collective-permute-start.20 = (bf16[192,1536]{1,0:T(8,128)(2,1)S(1)}, bf16[192,1536]{1,0:T(8,128)(2,1)S(1)}, u32[]{:S(2)}, u32[]{:S(2)}) collective-permute-start(bf16[192,1536]{1,0:T(8,128)(2,1)S(1)} %dynamic-slice_bitcast_fusion.6), channel_id=1, source_target_pairs={{0,8},{4,12},{8,0},{12,4},{1,9},{5,13},{9,1},{13,5},{2,10},{6,14},... | collective-permute-start | bytes 1769480 | tf_op jit(solution)/shard_map/ppermute | solution.py:965
  267.1 33.6 %collective-permute-start.35 = (bf16[2,384,768]{2,1,0:T(8,128)(2,1)}, bf16[2,384,768]{2,1,0:T(8,128)(2,1)}, u32[]{:S(2)}, u32[]{:S(2)}) collective-permute-start(bf16[2,384,768]{2,1,0:T(8,128)(2,1)} %dynamic-slice_bitcast_fusion), channel_id=1, source_target_pairs={{0,1},{1,0},{2,3},{3,2},{4,5},{5,4},{6,7},{7,6},{8,9},{9,8},{10,11... | collective-permute-start | bytes 3538952 | tf_op jit(solution)/shard_map/ppermute | solution.py:965
  273.0 2.5 copy-start.3
  275.6 1.2 slice-start
  277.9 22.7 %copy-start.5 = (bf16[1536,768]{1,0:T(8,128)(2,1)S(1)}, bf16[1536,768]{1,0:T(8,128)(2,1)}, u32[]{:S(2)}) copy-start(bf16[1536,768]{1,0:T(8,128)(2,1)} %shard_map.296) | copy-start | bytes 7077892
  278.1 33.2 %collective-permute-start.23 = (bf16[2,192,768]{2,1,0:T(8,128)(2,1)S(1)}, bf16[2,192,768]{2,1,0:T(8,128)(2,1)S(1)}, u32[]{:S(2)}, u32[]{:S(2)}) collective-permute-start(bf16[2,192,768]{2,1,0:T(8,128)(2,1)S(1)} %dynamic-slice_bitcast_fusion.4), channel_id=1, source_target_pairs={{0,1},{1,0},{2,3},{3,2},{4,5},{5,4},{6,7},{7,6},{8,9},{9,8},{10,11... | collective-permute-start | bytes 1769480 | tf_op jit(solution)/shard_map/ppermute | solution.py:965
  302.3 29.7 %collective-permute-start.36 = (bf16[384,768]{1,0:T(8,128)(2,1)S(1)}, bf16[384,768]{1,0:T(8,128)(2,1)S(1)}, u32[]{:S(2)}, u32[]{:S(2)}) collective-permute-start(bf16[384,768]{1,0:T(8,128)(2,1)S(1)} %dynamic-slice_bitcast_fusion.3), channel_id=1, source_target_pairs={{0,2},{1,3},{2,0},{3,1},{4,6},{5,7},{6,4},{7,5},{8,10},{9,11},{10,... | collective-permute-start | bytes 1769480 | tf_op jit(solution)/shard_map/ppermute | solution.py:965
  303.3 8.2 %copy-start.11 = (bf16[4,128,384]{2,1,0:T(8,128)(2,1)}, bf16[4,128,384]{2,1,0:T(8,128)(2,1)S(1)}, u32[]{:S(2)}) copy-start(bf16[4,128,384]{2,1,0:T(8,128)(2,1)S(1)} %bitcast_dynamic-update-slice_fusion) | copy-start | bytes 1179652
  311.5 26.8 %collective-permute-start.24 = (bf16[192,768]{1,0:T(8,128)(2,1)S(1)}, bf16[192,768]{1,0:T(8,128)(2,1)S(1)}, u32[]{:S(2)}, u32[]{:S(2)}) collective-permute-start(bf16[192,768]{1,0:T(8,128)(2,1)S(1)} %dynamic-slice_bitcast_fusion.7), channel_id=1, source_target_pairs={{0,2},{1,3},{2,0},{3,1},{4,6},{5,7},{6,4},{7,5},{8,10},{9,11},{10,... | collective-permute-start | bytes 884744 | tf_op jit(solution)/shard_map/ppermute | solution.py:965
  333.0 7.0 %collective-permute-start.37 = (bf16[192,768]{1,0:T(8,128)(2,1)S(1)}, bf16[192,768]{1,0:T(8,128)(2,1)S(1)}, u32[]{:S(2)}, u32[]{:S(2)}) collective-permute-start(bf16[192,768]{1,0:T(8,128)(2,1)S(1)} %get-tuple-element.102), channel_id=1, source_target_pairs={{0,0},{1,4},{2,8},{3,12},{4,1},{5,5},{6,9},{7,13},{8,2},{9,6},{10,... | collective-permute-start | bytes 884744 | tf_op jit(solution)/shard_map/ppermute | solution.py:1105
  338.3 2.5 copy-start.1
  (5 other events, 3.8 us)
